TPU v7x, 32 devices: a whole 2x2x4 slice. The times are simulated.
32 devices in a mesh: head: 2 (over y), blk: 16 (over z, x, core).
Axes of the slice: x: 2, y: 2, z: 4, core: 2. Of those that a mesh axis runs over, the one named last changes fastest.
Arguments:
- hidden_in: float32 [128, 1024], P('blk'), may hold values from -41 to 41
- attention_gain: float32 [1024], replicated, may hold values from 0.1 to 1.9
- mlp_gain: float32 [1024], replicated, may hold values from 0.1 to 1.9
- qkv_weight: bfloat16 [3, 1024, 1024], P(None, None, 'head'), may hold values from -1 to 1
- out_weight: bfloat16 [1024, 1024], P('head'), may hold values from -0.1875 to 0.1875
- up_weight: bfloat16 [1024, 4096], P(None, 'head'), may hold values from -0.1875 to 0.1875
- down_weight: bfloat16 [4096, 1024], P('head'), may hold values from -0.09375 to 0.09375
- position_bias: float32 [32, 16], P(None, 'head'), may hold values from -6 to 303
- bucket_edges: int32 [31], replicated, may hold values from 1 to 1035, as said below
- cache_keys: bfloat16 [384, 128, 1024], P('blk', None, 'head'), may hold values from -2 to 2
- cache_values: bfloat16 [384, 128, 1024], P('blk', None, 'head'), may hold values from -6 to 6
- lengths: int32 [128], replicated, may hold values from 1 to 16384, as said below
- page_request: int32 [384], P('blk'), may hold values from -1 to 127, as said below
- page_index: int32 [384], P('blk'), may hold values from 0 to 127, as said below
Outputs:
- new_hidden: float32 [128, 1024], P('blk', 'head')
Inputs may be any that keep to these rules, and one draw needn't show every extreme that they name: Request r holds lengths[r] cached tokens; for each k below ceil(lengths[r] / 128) exactly one slot s has page_request[s] = r and page_index[s] = k, and no other slot names r. Every request has at least one page; some request has 16384 tokens. `page_request`: -1 marks a free slot. A free slot has page_index 0. `bucket_edges`: strictly rising; its first 15 entries are 1, 2, 3 and so on.
All inputs are finite; a program needn't handle non-finite values.
Results may differ from a plain program's by a relative error of at most 0.009.
Values may be sent and summed in bfloat16 or wider, within the bound.
No kernel may reach another device: no remote copies, remote signals or barrier semaphores. Data moves between devices by JAX's collectives and lax.ppermute only.
A program may use at most 64 MiB of HBM per device.

v0:
```python
import functools

import jax
import jax.numpy as jnp
from jax import lax
from jax.experimental import pallas as pl
from jax.experimental.pallas import tpu as pltpu
from jax.sharding import PartitionSpec as P

HEAD_DIM = 64
PAGE = 128
LANES = 128

far_below = -1e30
epsilon = 1e-06

VMEM_SPEC = pl.BlockSpec(memory_space=pltpu.VMEM)
SMEM_SPEC = pl.BlockSpec(memory_space=pltpu.SMEM)
ANY_SPEC = pl.BlockSpec(memory_space=pl.ANY)
HBM_SPEC = pl.BlockSpec(memory_space=pltpu.HBM)
PARAMS = pltpu.CompilerParams(vmem_limit_bytes=16 * 1024 * 1024)

PIECE = 8
SUM_LANE = 3 * PIECE


def iota(shape, axis):
    return lax.broadcasted_iota(jnp.int32, shape, axis)


def split_index(x, size):
    if size & (size - 1):
        return lax.div(x, size), lax.rem(x, size)
    return x >> (size.bit_length() - 1), x & (size - 1)


def head_of(shape, axis):
    return split_index(iota(shape, axis), HEAD_DIM)[0]


def pieces(x, count):
    parts = []
    for _ in range(count):
        part = x.astype(jnp.bfloat16)
        parts.append(part)
        x = x - part.astype(jnp.float32)
    return parts


def rms_normed(x, gain):
    scale = lax.rsqrt(jnp.mean(x * x, axis=1, keepdims=True) + epsilon)
    return (x * scale * gain).astype(jnp.bfloat16)


def dot(a, b, dims=((1,), (0,)), precision=None):
    return lax.dot_general(
        a, b, (dims, ((), ())), preferred_element_type=jnp.float32, precision=precision
    )


def split_copies(source, target, sems, count):
    size = source.shape[0] // count
    return [
        pltpu.make_async_copy(
            source.at[pl.ds(i * size, size)], target.at[pl.ds(i * size, size)], sems.at[i]
        )
        for i in range(count)
    ]


def query_kernel(hidden_hbm, gain_hbm, weight_hbm, query_ref, hidden, gain, weight, sems):
    model = hidden.shape[1]
    small = [
        pltpu.make_async_copy(hidden_hbm, hidden, sems.at[0]),
        pltpu.make_async_copy(gain_hbm, gain, sems.at[1]),
    ]
    half = model // 4
    large = [
        pltpu.make_async_copy(
            weight_hbm.at[0, pl.ds(i * half, half)], weight.at[pl.ds(i * half, half)], sems.at[2 + i]
        )
        for i in range(4)
    ]
    for copy in small + large:
        copy.start()
    for copy in small:
        copy.wait()
    normed = rms_normed(hidden[...], gain[...])
    query = None
    for i, copy in enumerate(large):
        copy.wait()
        span = slice(i * half, (i + 1) * half)
        part = dot(normed[:, span], weight[span])
        query = part if query is None else query + part
    query_ref[...] = query.astype(jnp.bfloat16)


def page_kernel(
    own_rows, inner, outer, swapped, query_ref, request_ref, keys_hbm,
    keys_ref, pick_ref, place_ref, lead_ref, apart_ref, owners_ref,
    sems,
):
    copies = split_copies(
        keys_hbm.at[pl.ds(0, keys_ref.shape[0])], keys_ref, sems, sems.shape[0]
    )
    for copy in copies:
        copy.start()
    me = lax.axis_index("blk")
    page_count = apart_ref.shape[0]
    all_rows, depth = place_ref.shape
    page, lane = iota((page_count, page_count), 0), iota((page_count, page_count), 1)
    by_lane = request_ref[...]
    owner = jnp.max(jnp.where(page == lane, by_lane, -1), axis=1, keepdims=True)
    same = by_lane == owner
    apart_ref[...] = jnp.full(apart_ref.shape, 2 * far_below, jnp.float32)
    apart_ref[:, :page_count] = jnp.where(same, 0.0, 2 * far_below)
    earlier = jnp.max(jnp.where(same & (lane < page), 1, 0), axis=1, keepdims=True)
    lead_ref[...] = jnp.broadcast_to(jnp.where(earlier == 0, 1.0, 0.0), lead_ref.shape)
    owners_ref[...] = jnp.broadcast_to(owner, owners_ref.shape)
    device, own_row = split_index(jnp.maximum(owner, 0), own_rows)

    def slot_of(device):
        high, low = split_index(device ^ me, inner)
        low = jnp.where(high == 0, low, low ^ 1)
        low = -(low ^ (low >> 1)) & (inner - 1)
        slot = (low * outer + high) * own_rows + own_row
        return jnp.where(owner >= 0, slot, -1)

    slot = slot_of(device)
    sum_slot = slot_of(device ^ lax.axis_index("head")) if swapped else slot
    row_of = iota((page_count, all_rows), 1)
    picks = jnp.where(row_of == slot, 1.0, 0.0)
    picks = [jnp.broadcast_to(picks[p : p + 1], (PIECE, all_rows)) for p in range(page_count)]
    pick_ref[...] = jnp.concatenate(picks, axis=0).astype(jnp.bfloat16)
    mine = split_index(iota((page_count, depth), 1), PIECE)[0] == iota((page_count, depth), 0)
    row = iota((all_rows, depth), 0)
    spread = jnp.max(jnp.where(mine, sum_slot, -1), axis=0, keepdims=True)
    place_ref[...] = (row == spread).astype(jnp.bfloat16)
    for copy in copies:
        copy.wait()


def bias_kernel(
    table_hbm, edges_hbm, lengths_hbm, index_hbm, owners_ref, keys_hbm, after_ref,
    keys_ref, bias_ref,
    table, edges, lengths, index, small_sems, sems,
):
    sources, targets = (table_hbm, edges_hbm, lengths_hbm, index_hbm), (table, edges, lengths, index)
    small = [
        pltpu.make_async_copy(source, target, small_sems.at[i])
        for i, (source, target) in enumerate(zip(sources, targets))
    ]
    late = keys_ref.shape[0]
    copies = split_copies(
        keys_hbm.at[pl.ds(keys_hbm.shape[0] - late, late)], keys_ref, sems, sems.shape[0]
    )
    for copy in small + copies:
        copy.start()
    for copy in small:
        copy.wait()
    heads, buckets = table.shape
    page_count = index.shape[1]
    owner = owners_ref[:, 0:1]
    square = (page_count, page_count)
    number = jnp.where(iota(square, 0) == iota(square, 1), index[...], 0)
    number = jnp.sum(number, axis=1, keepdims=True)
    requests = lengths.shape[1]
    length = jnp.where(iota((page_count, requests), 1) == owner, lengths[...], 0)
    length = jnp.sum(length, axis=1, keepdims=True)
    distance = length - number * PAGE - iota((page_count, PAGE), 1)
    far = [distance >= edges[k] for k in range(buckets - 1)]
    usable = (owner >= 0) & (distance > 0)
    bias_ref[...] = jnp.full(bias_ref.shape, far_below, jnp.float32)
    for h in range(heads):
        bias = jnp.full((page_count, PAGE), table[h, 0], jnp.float32)
        for k in range(buckets - 1):
            bias = jnp.where(far[k], table[h, k + 1], bias)
        bias_ref[pl.ds(h, page_count, stride=PIECE), :] = jnp.where(usable, bias, far_below)
    for copy in copies:
        copy.wait()


def side_kernel(
    hidden_ref, gain_ref, query_ref, table_ref, weight_hbm, out_hbm, after_ref,
    fresh_ref, out_ref, spread_ref,
    weight, weight_sems, sems,
):
    copies = [
        pltpu.make_async_copy(weight_hbm.at[1 + i], weight.at[i], weight_sems.at[i])
        for i in range(2)
    ]
    later = split_copies(out_hbm, out_ref, sems, sems.shape[0])
    for copy in copies + later:
        copy.start()
    normed = rms_normed(hidden_ref[...], gain_ref[...])
    heads = table_ref.shape[0]
    spread = iota((heads, LANES), 0) == iota((heads, LANES), 1)
    score = jnp.sum(jnp.where(spread, table_ref[:, 0:1], 0.0), axis=0, keepdims=True)
    copies[0].wait()
    key = dot(normed, weight[0]).astype(jnp.bfloat16)
    product = query_ref[...].astype(jnp.float32) * key.astype(jnp.float32)
    width = product.shape[1]
    gather = (head_of((width, LANES), 0) == iota((width, LANES), 1)).astype(jnp.bfloat16)
    for part in pieces(product, 2):
        score = score + dot(part, gather)
    lane = iota(score.shape, 1)
    used = width // HEAD_DIM
    peak = jnp.where(lane < used, score, 0.0)
    total = jnp.where((lane >= SUM_LANE) & (lane < SUM_LANE + used), 1.0, 0.0)
    fresh_ref[:, width:] = packed_stats(peak, total)
    spread = (iota((LANES, width), 0) == head_of((LANES, width), 1)).astype(jnp.bfloat16)
    spread_ref[:LANES] = spread
    spread_ref[LANES:] = spread
    copies[1].wait()
    fresh_ref[:, :width] = dot(normed, weight[1]).astype(jnp.bfloat16)
    for copy in later:
        copy.wait()


def load_kernel(start, source, after_ref, target, sems):
    rows = source.at[pl.ds(start, target.shape[0])]
    copies = split_copies(rows, target, sems, sems.shape[0])
    for copy in copies:
        copy.start()
    for copy in copies:
        copy.wait()


def packed_stats(peaks, sums):
    one, two, three = (part.astype(jnp.float32) for part in pieces(peaks + sums, 3))
    packed = one + pltpu.roll(two, PIECE, 1) + pltpu.roll(three, 2 * PIECE, 1)
    return packed.astype(jnp.bfloat16)


def unpacked_stats(packed, heads):
    stats = packed.astype(jnp.float32)
    stats = stats + pltpu.roll(stats, LANES - PIECE, 1) + pltpu.roll(stats, LANES - 2 * PIECE, 1)
    sums = pltpu.roll(stats, LANES - SUM_LANE, 1)
    used = iota(stats.shape, 1) < heads
    return jnp.where(used & (sums > 0.0), stats, far_below), jnp.where(used, sums, 0.0)


def over_columns(values, spread):
    return dot(jnp.concatenate(pieces(values, 2), axis=1), spread)


def attend_kernel(groups, *refs):
    query_refs, refs, sums_refs = refs[:groups], refs[groups:-groups], refs[-groups:]
    bias_ref, pick_ref, place_ref, lead_ref, apart_ref, keys_ref, late_ref, values_ref = refs
    page_count = apart_ref.shape[0]
    width = keys_ref.shape[2]
    early = keys_ref.shape[0]
    chunk = 2
    chunks = page_count // chunk
    queries = jnp.concatenate([ref[...] for ref in query_refs], axis=0)
    own_head = (head_of((PIECE, width), 1) == iota((PIECE, width), 0)).astype(jnp.float32)
    pair_heads = jnp.concatenate([own_head] * chunk, axis=0)
    chosen = dot(pick_ref[...], queries)
    lane = iota((PIECE, LANES), 1)
    row = iota((PIECE, LANES), 0)
    nothing = jnp.zeros((PIECE, PAGE), jnp.float32)
    raws = []
    for c in range(chunks):
        rows = chosen[c * chunk * PIECE : (c + 1) * chunk * PIECE]
        split = rows.astype(jnp.bfloat16) * pair_heads.astype(jnp.bfloat16)
        at = c * chunk
        block = keys_ref[at : at + chunk] if at < early else late_ref[at - early : at - early + chunk]
        raws.append(dot(split, block.reshape(chunk * PAGE, width), ((1,), (1,))))
    scores, page_tops = [], []
    for p in range(page_count):
        i = p % chunk
        part = raws[p // chunk][i * PIECE : (i + 1) * PIECE, i * PAGE : (i + 1) * PAGE]
        score = part + bias_ref[p * PIECE : (p + 1) * PIECE]
        scores.append(score)
        page_tops.append(jnp.max(score, axis=1, keepdims=True))
    page_weights = [jnp.exp(score - top) for score, top in zip(scores, page_tops)]
    mixes = []
    for c in range(chunks):
        blocks = []
        for i in range(chunk):
            weight = page_weights[c * chunk + i]
            blocks.append(
                jnp.concatenate([weight if k == i else nothing for k in range(chunk)], axis=1)
            )
        weights = jnp.concatenate(blocks, axis=0).astype(jnp.bfloat16)
        block = values_ref[c * chunk : (c + 1) * chunk]
        mixes.append(dot(weights, block.reshape(chunk * PAGE, width)))
    totals = [jnp.sum(weight, axis=1, keepdims=True) for weight in page_weights]
    tops = jnp.zeros((PIECE, LANES), jnp.float32)
    for p in range(page_count):
        tops = jnp.where(lane == p, page_tops[p], tops)
    stats = []
    for c in range(chunks):
        factors = []
        for p in range(c * chunk, (c + 1) * chunk):
            peak = jnp.max(tops + apart_ref[p : p + 1], axis=1, keepdims=True)
            factor = jnp.exp(page_tops[p] - peak)
            total = jnp.where(lane == row + SUM_LANE, totals[p] * factor, 0.0)
            stats.append(jnp.where(lane == row, peak * lead_ref[p : p + 1], total))
            factors.append(factor)
        mixes[c] = mixes[c] * (pair_heads * jnp.concatenate(factors, axis=0))
    mix = jnp.concatenate(mixes, axis=0).astype(jnp.bfloat16)
    stats = pieces(jnp.concatenate(stats, axis=0), 3)
    sums = dot(place_ref[...], jnp.concatenate([mix] + stats, axis=1))
    stats = sum(sums[:, width + i * LANES : width + (i + 1) * LANES] for i in range(3))
    stats = packed_stats(stats, 0.0).astype(jnp.float32)
    size = sums.shape[0] // groups
    for i, sums_ref in enumerate(sums_refs):
        first, middle, last = i * size, i * size + size // 2, (i + 1) * size
        for c in range(width // LANES):
            block = sums[first:last, c * LANES : (c + 1) * LANES]
            sums_ref[c * size : (c + 1) * size] = block.astype(jnp.bfloat16)
        both = stats[first:middle] + pltpu.roll(stats[middle:last], LANES // 2, 1)
        sums_ref[width // LANES * size :] = both.astype(jnp.bfloat16)


def combine_kernel(sources, *refs):
    part_refs, spread_ref, sums_refs = refs[:sources], refs[sources], refs[sources + 1 :]
    width = spread_ref.shape[1]
    rows = sum(ref.shape[0] for ref in sums_refs)
    heads, blocks = width // HEAD_DIM, width // LANES
    stats, mixes = [], []
    for ref in part_refs:
        both = ref[blocks * rows :].astype(jnp.float32)
        both = jnp.concatenate([both, pltpu.roll(both, LANES // 2, 1)], axis=0)
        stats.append(unpacked_stats(both, heads))
        mix = [ref[c * rows : (c + 1) * rows] for c in range(blocks)]
        mixes.append(jnp.concatenate(mix, axis=1).astype(jnp.float32))
    peak = stats[0][0]
    for peaks, _ in stats[1:]:
        peak = jnp.maximum(peak, peaks)
    factors = [jnp.exp(peaks - peak) for peaks, _ in stats]
    total = sum(factor * sums for factor, (_, sums) in zip(factors, stats))
    shares = over_columns(jnp.concatenate(factors, axis=0), spread_ref[...])
    mixed = sum(mix * shares[i * rows : (i + 1) * rows] for i, mix in enumerate(mixes))
    packed = packed_stats(
        jnp.where(total > 0.0, peak, 0.0), pltpu.roll(total, SUM_LANE, 1)
    ).astype(jnp.float32)
    size = sums_refs[0].shape[0]
    for i, sums_ref in enumerate(sums_refs):
        span = slice(i * size, (i + 1) * size)
        sums_ref[:, :width] = mixed[span].astype(jnp.bfloat16)
        sums_ref[:, width:] = packed[span].astype(jnp.bfloat16)


def merge_kernel(
    swapped, sources, hidden_ref, fresh_ref, moved_ref, weight_ref, spread_ref, *refs
):
    part_refs, (own_ref, send_ref) = refs[:sources], refs[sources:]
    width = fresh_ref.shape[1] - LANES
    heads = width // HEAD_DIM
    parts = [ref[...].astype(jnp.float32) for ref in part_refs]
    fresh = fresh_ref[...].astype(jnp.float32)
    if swapped:
        first = lax.axis_index("head") == 0
        fresh = jnp.where(first, fresh, moved_ref[...].astype(jnp.float32))
    parts.append(fresh)
    stats = [unpacked_stats(part[:, width:], heads) for part in parts]
    peak = stats[0][0]
    for peaks, _ in stats[1:]:
        peak = jnp.maximum(peak, peaks)
    factors = [jnp.exp(peaks - peak) for peaks, _ in stats]
    total = sum(factor * sums for factor, (_, sums) in zip(factors, stats))
    total = jnp.where(total > 0.0, total, 1.0)
    shares = jnp.concatenate([f / total for f in factors], axis=0)
    shares = over_columns(shares, spread_ref[...])
    rows = fresh_ref.shape[0]
    mixed = sum(
        part[:, :width] * shares[i * rows : (i + 1) * rows] for i, part in enumerate(parts)
    )
    projected = dot(mixed.astype(jnp.bfloat16), weight_ref[...])
    if swapped:
        projected = projected + jnp.where(first, hidden_ref[...], 0.0)
        own_ref[...] = projected
        both = [part.astype(jnp.float32) for part in pieces(projected, 2)]
        send_ref[...] = jnp.concatenate(both, axis=0).astype(jnp.bfloat16)
    else:
        own_ref[...] = hidden_ref[...]
        send_ref[...] = projected.astype(jnp.bfloat16)


def mlp_kernel(
    exchanged, own_ref, other_ref, gain_ref, up_ref, down_ref, late_ref, *outs
):
    other = other_ref[...].astype(jnp.float32)
    rows = own_ref.shape[0]
    middle = own_ref[...]
    for at in range(0, other.shape[0], rows):
        middle = middle + other[at : at + rows]
    normed = rms_normed(middle, gain_ref[...])
    active = jnp.maximum(dot(normed, up_ref[...]), 0.0).astype(jnp.bfloat16)
    half = down_ref.shape[0]
    down = dot(active[:, :half], down_ref[...]) + dot(active[:, half:], late_ref[...])
    if exchanged:
        kept_ref, sent_ref = outs
        columns = kept_ref.shape[1]
        low = lax.axis_index("head") == 0
        left, right = slice(0, columns), slice(columns, 2 * columns)
        kept = middle + down

        @pl.when(low)
        def _():
            kept_ref[...] = kept[:, left]
            sent_ref[...] = down[:, right]

        @pl.when(jnp.logical_not(low))
        def _():
            kept_ref[...] = kept[:, right]
            sent_ref[...] = down[:, left]

    else:
        middle_ref, down_out_ref = outs
        middle_ref[...] = middle
        down_out_ref[...] = down.astype(jnp.bfloat16)


def loading(*arrays):
    return pl.CostEstimate(
        flops=0, bytes_accessed=sum(2 * array.size for array in arrays), transcendentals=0
    )


def in_hbm(*arrays):
    return [pltpu.with_memory_space_constraint(array, pltpu.HBM) for array in arrays]


def xor_pairs(size, step):
    return [(i, i ^ step) for i in range(size)]


def per_device(
    hidden_in, attention_gain, mlp_gain, qkv_weight, out_weight, up_weight, down_weight,
    position_bias, bucket_edges, cache_keys, cache_values, lengths, page_request, page_index,
):
    f32, bf16 = jnp.float32, jnp.bfloat16
    shape = jax.ShapeDtypeStruct
    own_rows, model = hidden_in.shape
    width = qkv_weight.shape[2]
    page_count = page_request.shape[0]
    blocks = lax.axis_size("blk")
    all_rows = own_rows * blocks
    halves = lax.axis_size("head")
    columns = model // halves
    exchanged = halves == 2
    gain = attention_gain.reshape(1, model)
    query = pl.pallas_call(
        query_kernel,
        out_shape=shape((own_rows, width), bf16),
        in_specs=[HBM_SPEC] * 3,
        out_specs=VMEM_SPEC,
        scratch_shapes=[
            pltpu.VMEM((own_rows, model), f32),
            pltpu.VMEM((1, model), f32),
            pltpu.VMEM((model, width), bf16),
            pltpu.SemaphoreType.DMA((6,)),
        ],
        compiler_params=PARAMS,
        name="query",
    )(*in_hbm(hidden_in, gain, qkv_weight))

    inner = 1
    while inner * inner < blocks:
        inner *= 2
    far = [query] + [
        lax.ppermute(query, "blk", xor_pairs(blocks, step * inner ^ 1))
        for step in range(1, blocks // inner)
    ]
    depth = page_count * PIECE
    early = page_count // 6 * 2
    keys, picks, place, leads, apart, owners = pl.pallas_call(
        functools.partial(page_kernel, own_rows, inner, blocks // inner, exchanged),
        out_shape=(
            pltpu.VMEM((early,) + cache_keys.shape[1:], bf16),
            shape((depth, all_rows), bf16),
            shape((all_rows, depth), bf16),
            shape((page_count, LANES), f32),
            shape((page_count, LANES), f32),
            shape((page_count, LANES), jnp.int32),
        ),
        in_specs=[ANY_SPEC, VMEM_SPEC, HBM_SPEC],
        out_specs=(VMEM_SPEC,) * 6,
        scratch_shapes=[pltpu.SemaphoreType.DMA((4,))],
        compiler_params=PARAMS,
        cost_estimate=loading(cache_keys),
        name="pages",
    )(query, page_request.reshape(1, page_count), *in_hbm(cache_keys))
    near, apart = lax.optimization_barrier((jnp.concatenate(far, axis=0), apart))
    steps = sorted(range(inner), key=lambda step: -(step ^ (step >> 1)) & (inner - 1))
    gathered = [near] + [lax.ppermute(near, "blk", xor_pairs(blocks, step)) for step in steps[1:]]
    table = position_bias.T
    late_keys, bias = pl.pallas_call(
        bias_kernel,
        out_shape=(
            pltpu.VMEM((page_count - early,) + cache_keys.shape[1:], bf16),
            shape((depth, PAGE), f32),
        ),
        in_specs=[HBM_SPEC] * 4 + [VMEM_SPEC, HBM_SPEC, ANY_SPEC],
        out_specs=(VMEM_SPEC,) * 2,
        scratch_shapes=[
            pltpu.SMEM(table.shape, f32),
            pltpu.SMEM(bucket_edges.shape, jnp.int32),
            pltpu.VMEM((1,) + lengths.shape, jnp.int32),
            pltpu.VMEM((1,) + page_index.shape, jnp.int32),
            pltpu.SemaphoreType.DMA((4,)),
            pltpu.SemaphoreType.DMA((4,)),
        ],
        compiler_params=PARAMS,
        cost_estimate=loading(cache_values),
        name="bias",
    )(
        *in_hbm(table, bucket_edges, lengths[None], page_index[None]), owners,
        *in_hbm(cache_keys), near,
    )

    groups = len(gathered)
    size = all_rows // groups
    message = width // LANES * size + size // 2
    sums = pl.pallas_call(
        functools.partial(attend_kernel, groups),
        out_shape=(shape((message, LANES), bf16),) * groups,
        in_specs=[VMEM_SPEC] * (groups + 8),
        out_specs=(VMEM_SPEC,) * groups,
        compiler_params=PARAMS,
        name="attend",
    )(*gathered, bias, picks, place, leads, apart, keys, late_keys, cache_values)
    near_sums = [sums[0]] + [
        lax.ppermute(sums[i], "blk", xor_pairs(blocks, steps[i]))
        for i in range(1, inner)
    ]

    fresh, out_near, spread = pl.pallas_call(
        side_kernel,
        out_shape=(
            shape((own_rows, width + LANES), bf16),
            pltpu.VMEM(out_weight.shape, bf16),
            shape((2 * LANES, width), bf16),
        ),
        in_specs=[VMEM_SPEC] * 4 + [HBM_SPEC] * 2 + [ANY_SPEC],
        out_specs=(VMEM_SPEC,) * 3,
        scratch_shapes=[
            pltpu.VMEM((2, model, width), bf16),
            pltpu.SemaphoreType.DMA((2,)),
            pltpu.SemaphoreType.DMA((4,)),
        ],
        compiler_params=PARAMS,
        cost_estimate=loading(out_weight, out_weight, out_weight),
        name="side",
    )(
        hidden_in, gain, query, table,
        *in_hbm(qkv_weight, out_weight), sums[0],
    )

    *near_sums, fresh = lax.optimization_barrier((*near_sums, fresh))
    outer = blocks // inner
    sums = pl.pallas_call(
        functools.partial(combine_kernel, inner),
        out_shape=(shape((own_rows, width + LANES), bf16),) * outer,
        in_specs=[VMEM_SPEC] * (inner + 1),
        out_specs=(VMEM_SPEC,) * outer,
        compiler_params=PARAMS,
        name="combine",
    )(*near_sums, spread)
    units = down_weight.shape[0]
    cut = units // 8 * 3

    def load_down(start, stop, after):
        return pl.pallas_call(
            functools.partial(load_kernel, start),
            out_shape=pltpu.VMEM((stop - start, model), bf16),
            in_specs=[HBM_SPEC, ANY_SPEC],
            out_specs=VMEM_SPEC,
            scratch_shapes=[pltpu.SemaphoreType.DMA((4,))],
            compiler_params=PARAMS,
            cost_estimate=loading(down_weight),
            name="load",
        )(*in_hbm(down_weight), after)

    down_early = load_down(0, cut, sums[0])
    parts = [sums[0]] + [
        lax.ppermute(sums[step], "blk", xor_pairs(blocks, step * inner ^ 1))
        for step in reversed(range(1, outer))
    ]

    moved = lax.ppermute(fresh, "blk", xor_pairs(blocks, 1)) if exchanged else fresh
    *parts, down_early = lax.optimization_barrier((*parts, down_early))
    own_part, sent_part = pl.pallas_call(
        functools.partial(merge_kernel, exchanged, outer),
        out_shape=(
            shape((own_rows, model), f32),
            shape(((2 if exchanged else 1) * own_rows, model), bf16),
        ),
        in_specs=[VMEM_SPEC] * (outer + 5),
        out_specs=(VMEM_SPEC,) * 2,
        compiler_params=PARAMS,
        name="merge",
    )(hidden_in, fresh, moved, out_near, spread, *parts)

    down_late = load_down(cut, units, sent_part)
    axes = ("head", "blk")
    across = [(i, blocks + (i ^ 1)) for i in range(blocks)]
    back = [(b, a) for a, b in across]
    if exchanged:
        other_part = lax.ppermute(sent_part, axes, across + back)
        mlp_out = (shape((own_rows, columns), f32), shape((own_rows, columns), f32))
    else:
        other_part = lax.psum(sent_part, "head")
        mlp_out = (shape((own_rows, model), f32), shape((own_rows, model), bf16))

    kept, leaving = pl.pallas_call(
        functools.partial(mlp_kernel, exchanged),
        out_shape=mlp_out,
        in_specs=[VMEM_SPEC] * 6,
        out_specs=(VMEM_SPEC,) * 2,
        compiler_params=PARAMS,
        name="mlp",
    )(own_part, other_part, mlp_gain.reshape(1, model), up_weight, down_early, down_late)

    if exchanged:
        straight = [(i, blocks + i) for i in range(blocks)]
        arrived = lax.ppermute(leaving, axes, straight + back)
        moved = lax.ppermute(kept, "blk", xor_pairs(blocks, 1))
        kept = jnp.where(lax.axis_index("head") == 0, kept, moved)
    else:
        kept = lax.dynamic_slice_in_dim(kept, lax.axis_index("head") * columns, columns, 1)
        arrived = lax.psum_scatter(leaving, "head", scatter_dimension=1, tiled=True)
    return kept + arrived.astype(f32)


def solution(mesh):
    in_specs = (
        P("blk", None),
        P(),
        P(),
        P(None, None, "head"),
        P("head", None),
        P(None, "head"),
        P("head", None),
        P(None, "head"),
        P(),
        P("blk", None, "head"),
        P("blk", None, "head"),
        P(),
        P("blk"),
        P("blk"),
    )
    out_specs = P("blk", "head")
    return jax.shard_map(
        per_device, mesh=mesh, in_specs=in_specs, out_specs=out_specs, check_vma=False
    )
```

profile of v0, /device:TPU:0, one launch (start us, length us, event | category | flops | bytes accessed | tf_op | source)
XLA Modules:
  0.0 36.5 jit_solution(6242601484451280057)
XLA Ops:
  0.0 0.0 copy-start.6
  0.0 1.4 %query.1.query_ref = bf16[8,512]{1,0:T(8,128)(2,1)S(1)} custom-call(f32[8,1024]{1,0:T(8,128)} %hidden_ref.3, f32[1,1024]{1,0:T(1,128)} %bitcast.6, bf16[3,1024,512]{2,1,0:T(8,128)(2,1)} %weight_hbm.3), custom_call_target="tpu_custom_call" | custom-call | tf_op jit(solution)/shard_map/query/pallas_call | solution.py:446
  1.4 4.6 %collective-permute-start.2 = (bf16[8,512]{1,0:T(8,128)(2,1)S(1)}, bf16[8,512]{1,0:T(8,128)(2,1)S(1)}, u32[]{:S(2)}, u32[]{:S(2)}) collective-permute-start(bf16[8,512]{1,0:T(8,128)(2,1)S(1)} %query.1.query_ref), channel_id=1, source_target_pairs={{0,13},{1,12},{2,15},{3,14},{4,9},{5,8},{6,11},{7,10},{8,5},{9,4},... | collective-permute-start | bytes 24584 | tf_op jit(solution)/shard_map/ppermute | solution.py:465
  6.0 0.0 collective-permute-start.1
  6.0 0.9 %collective-permute-start = (bf16[8,512]{1,0:T(8,128)(2,1)S(1)}, bf16[8,512]{1,0:T(8,128)(2,1)S(1)}, u32[]{:S(2)}, u32[]{:S(2)}) collective-permute-start(bf16[8,512]{1,0:T(8,128)(2,1)S(1)} %query.1.query_ref), channel_id=1, source_target_pairs={{0,5},{1,4},{2,7},{3,6},{4,1},{5,0},{6,3},{7,2},{8,13},{9,12},{10,... | collective-permute-start | bytes 24584 | tf_op jit(solution)/shard_map/ppermute | solution.py:465
  6.9 0.0 copy-done.6
  6.9 0.0 copy-start.1
  6.9 1.4 %pages.1 = (bf16[8,128,512]{2,1,0:T(8,128)(2,1)S(1)}, bf16[192,128]{1,0:T(8,128)(2,1)S(1)}, bf16[128,192]{1,0:T(8,128)(2,1)S(1)}, f32[24,128]{1,0:T(8,128)S(1)},...) custom-call(bf16[8,512]{1,0:T(8,128)(2,1)S(1)} %query.1.query_ref, s32[1,24]{1,0:T(1,128)S(1)} %bitcast.11, ...), custom_call_target="tpu_custom_call" | custom-call | bytes 3145728 | tf_op jit(solution)/shard_map/pages/pallas_call | solution.py:470
  8.3 0.0 collective-permute-done.2
  8.3 1.7 %collective-permute-done.1 = bf16[8,512]{1,0:T(8,128)(2,1)S(1)} collective-permute-done((bf16[8,512]{1,0:T(8,128)(2,1)S(1)}, bf16[8,512]{1,0:T(8,128)(2,1)S(1)}, u32[]{:S(2)}, u32[]{:S(2)}) %collective-permute-start.1) | collective-permute-done | bytes 8224 | tf_op jit(solution)/shard_map/ppermute | solution.py:465
  10.0 0.0 collective-permute-done
  10.0 1.5 %collective-permute-start.3 = (bf16[32,512]{1,0:T(8,128)(2,1)S(1)}, bf16[32,512]{1,0:T(8,128)(2,1)S(1)}, u32[]{:S(2)}, u32[]{:S(2)}) collective-permute-start(bf16[32,512]{1,0:T(8,128)(2,1)S(1)} %pad_maximum_fusion.after_ref.refs_0_), channel_id=1, source_target_pairs={{0,2},{1,3},{2,0},{3,1},{4,6},{5,7},{6,4},{7,5},{8,10},{9,11},{10,... | collective-permute-start | bytes 98312 | tf_op jit(solution)/shard_map/ppermute | solution.py:489
  11.5 0.5 %collective-permute-start.4 = (bf16[32,512]{1,0:T(8,128)(2,1)S(1)}, bf16[32,512]{1,0:T(8,128)(2,1)S(1)}, u32[]{:S(2)}, u32[]{:S(2)}) collective-permute-start(bf16[32,512]{1,0:T(8,128)(2,1)S(1)} %pad_maximum_fusion.after_ref.refs_0_), channel_id=1, source_target_pairs={{0,3},{1,2},{2,1},{3,0},{4,7},{5,6},{6,5},{7,4},{8,11},{9,10},{10,... | collective-permute-start | bytes 98312 | tf_op jit(solution)/shard_map/ppermute | solution.py:489
  12.0 0.2 collective-permute-start.5
  12.2 1.6 %bias.1 = (bf16[16,128,512]{2,1,0:T(8,128)(2,1)S(1)}, f32[192,128]{1,0:T(8,128)S(1)}) custom-call(f32[8,32]{1,0:T(8,128)} %bitcast.8, s32[31]{0:T(128)} %edges_hbm.1, s32[1,128]{1,0:T(1,128)} %bitcast.12, s32[1,24]{1,0:T(1,128)} %bitcast.13, s32[24,128]{1,0:T(8,128)S(1)} %get-tuple-element.42.owners_ref, bf16[24,128,512]{2,1,0:T(8,128)(2,1)} %keys_hbm.3, ...), custom_call_target="tpu_custom_call" | custom-call | bytes 3145728 | tf_op jit(solution)/shard_map/bias/pallas_call | solution.py:491
  13.8 0.2 collective-permute-done.3.refs_1_
  14.0 0.9 %collective-permute-done.4.refs_2_ = bf16[32,512]{1,0:T(8,128)(2,1)S(1)} collective-permute-done((bf16[32,512]{1,0:T(8,128)(2,1)S(1)}, bf16[32,512]{1,0:T(8,128)(2,1)S(1)}, u32[]{:S(2)}, u32[]{:S(2)}) %collective-permute-start.4) | collective-permute-done | bytes 32800 | tf_op jit(solution)/shard_map/ppermute | solution.py:489
  14.9 0.0 collective-permute-done.5.refs_3_
  14.9 0.0 copy-done.1
  14.9 0.0 copy-start.2
  14.9 0.0 copy-start.3
  14.9 0.0 copy-start.4
  14.9 1.8 %attend.1 = (bf16[144,128]{1,0:T(8,128)(2,1)S(1)}, bf16[144,128]{1,0:T(8,128)(2,1)S(1)}, bf16[144,128]{1,0:T(8,128)(2,1)S(1)}, bf16[144,128]{1,0:T(8,128)(2,1)S(1)}) custom-call(bf16[32,512]{1,0:T(8,128)(2,1)S(1)} %pad_maximum_fusion.after_ref.refs_0_, bf16[32,512]{1,0:T(8,128)(2,1)S(1)} %collective-permute-done.3.refs_1_, ...), custom_call_target="tpu_custom_call" | custom-call | tf_op jit(solution)/shard_map/attend/pallas_call | solution.py:518
  16.7 1.0 %collective-permute-start.6 = (bf16[144,128]{1,0:T(8,128)(2,1)S(1)}, bf16[144,128]{1,0:T(8,128)(2,1)S(1)}, u32[]{:S(2)}, u32[]{:S(2)}) collective-permute-start(bf16[144,128]{1,0:T(8,128)(2,1)S(1)} %get-tuple-element.51), channel_id=1, source_target_pairs={{0,2},{1,3},{2,0},{3,1},{4,6},{5,7},{6,4},{7,5},{8,10},{9,11},{10,... | collective-permute-start | bytes 110600 | tf_op jit(solution)/shard_map/ppermute | solution.py:527
  17.7 0.8 %collective-permute-start.7 = (bf16[144,128]{1,0:T(8,128)(2,1)S(1)}, bf16[144,128]{1,0:T(8,128)(2,1)S(1)}, u32[]{:S(2)}, u32[]{:S(2)}) collective-permute-start(bf16[144,128]{1,0:T(8,128)(2,1)S(1)} %get-tuple-element.52), channel_id=1, source_target_pairs={{0,3},{1,2},{2,1},{3,0},{4,7},{5,6},{6,5},{7,4},{8,11},{9,10},{10,... | collective-permute-start | bytes 110600 | tf_op jit(solution)/shard_map/ppermute | solution.py:527
  18.4 0.4 %collective-permute-start.8 = (bf16[144,128]{1,0:T(8,128)(2,1)S(1)}, bf16[144,128]{1,0:T(8,128)(2,1)S(1)}, u32[]{:S(2)}, u32[]{:S(2)}) collective-permute-start(bf16[144,128]{1,0:T(8,128)(2,1)S(1)} %get-tuple-element.53), channel_id=1, source_target_pairs={{0,1},{1,0},{2,3},{3,2},{4,5},{5,4},{6,7},{7,6},{8,9},{9,8},{10,11... | collective-permute-start | bytes 110600 | tf_op jit(solution)/shard_map/ppermute | solution.py:527
  18.9 0.0 copy-done.2
  18.9 0.0 copy-done.3
  18.9 0.0 copy-done.4
  18.9 2.2 %side.1 = (bf16[8,640]{1,0:T(8,128)(2,1)S(1)}, bf16[512,1024]{1,0:T(8,128)(2,1)S(1)}, bf16[256,512]{1,0:T(8,128)(2,1)S(1)}) custom-call(f32[8,1024]{1,0:T(8,128)S(1)} %copy-done.2, f32[1,1024]{1,0:T(1,128)S(1)} %bitcast.7, bf16[8,512]{1,0:T(8,128)(2,1)S(1)} %query.1.query_ref, f32[8,32]{1,0:T(8,128)S(1)} %bitcast.9, bf16[3,1024,512]{2,1,0:T(8,128)(2,1)} %weight_hbm.3, ...), custom_call_target="tpu_custom_call" | custom-call | bytes 3145728 | tf_op jit(solution)/shard_map/side/pallas_call | solution.py:531
  21.0 0.0 collective-permute-done.6.refs_1_
  21.1 0.3 collective-permute-done.7.refs_2_
  21.3 0.0 collective-permute-done.8.refs_3_
  21.3 0.4 %combine.1 = (bf16[8,640]{1,0:T(8,128)(2,1)S(1)}, bf16[8,640]{1,0:T(8,128)(2,1)S(1)}, bf16[8,640]{1,0:T(8,128)(2,1)S(1)}, bf16[8,640]{1,0:T(8,128)(2,1)S(1)}) custom-call(bf16[144,128]{1,0:T(8,128)(2,1)S(1)} %get-tuple-element.58.after_ref.refs_0_, bf16[144,128]{1,0:T(8,128)(2,1)S(1)} %collective-permute-done.6.refs_1_, ...), custom_call_target="tpu_custom_call" | custom-call | tf_op jit(solution)/shard_map/combine/pallas_call | solution.py:555
  21.7 1.5 %collective-permute-start.10 = (bf16[8,640]{1,0:T(8,128)(2,1)S(1)}, bf16[8,640]{1,0:T(8,128)(2,1)S(1)}, u32[]{:S(2)}, u32[]{:S(2)}) collective-permute-start(bf16[8,640]{1,0:T(8,128)(2,1)S(1)} %get-tuple-element.63), channel_id=1, source_target_pairs={{0,13},{1,12},{2,15},{3,14},{4,9},{5,8},{6,11},{7,10},{8,5},{9,4},... | collective-permute-start | bytes 30728 | tf_op jit(solution)/shard_map/ppermute | solution.py:580
  23.3 0.8 %collective-permute-start.11 = (bf16[8,640]{1,0:T(8,128)(2,1)S(1)}, bf16[8,640]{1,0:T(8,128)(2,1)S(1)}, u32[]{:S(2)}, u32[]{:S(2)}) collective-permute-start(bf16[8,640]{1,0:T(8,128)(2,1)S(1)} %get-tuple-element.64), channel_id=1, source_target_pairs={{0,9},{1,8},{2,11},{3,10},{4,13},{5,12},{6,15},{7,14},{8,1},{9,0},... | collective-permute-start | bytes 30728 | tf_op jit(solution)/shard_map/ppermute | solution.py:580
  24.1 1.5 %collective-permute-start.12 = (bf16[8,640]{1,0:T(8,128)(2,1)S(1)}, bf16[8,640]{1,0:T(8,128)(2,1)S(1)}, u32[]{:S(2)}, u32[]{:S(2)}) collective-permute-start(bf16[8,640]{1,0:T(8,128)(2,1)S(1)} %get-tuple-element.65), channel_id=1, source_target_pairs={{0,5},{1,4},{2,7},{3,6},{4,1},{5,0},{6,3},{7,2},{8,13},{9,12},{10,... | collective-permute-start | bytes 30728 | tf_op jit(solution)/shard_map/ppermute | solution.py:580
  25.6 0.4 %collective-permute-start.9 = (bf16[8,640]{1,0:T(8,128)(2,1)S(1)}, bf16[8,640]{1,0:T(8,128)(2,1)S(1)}, u32[]{:S(2)}, u32[]{:S(2)}) collective-permute-start(bf16[8,640]{1,0:T(8,128)(2,1)S(1)} %get-tuple-element.55.fresh_ref), channel_id=1, source_target_pairs={{0,1},{1,0},{2,3},{3,2},{4,5},{5,4},{6,7},{7,6},{8,9},{9,8},{10,11... | collective-permute-start | bytes 30728 | tf_op jit(solution)/shard_map/ppermute | solution.py:584
  26.1 1.4 %load.2.down_ref = bf16[768,1024]{1,0:T(8,128)(2,1)S(1)} custom-call(bf16[2048,1024]{1,0:T(8,128)(2,1)} %source.3, bf16[8,640]{1,0:T(8,128)(2,1)S(1)} %get-tuple-element.66.after_ref.refs_0_), custom_call_target="tpu_custom_call" | custom-call | bytes 4194304 | tf_op jit(solution)/shard_map/load/pallas_call | solution.py:567
  27.4 0.0 collective-permute-done.10.refs_1_
  27.5 0.0 collective-permute-done.11.refs_2_
  27.5 0.0 collective-permute-done.12.refs_3_
  27.5 0.0 collective-permute-done.9.moved_ref
  27.5 0.5 %merge.1 = (f32[8,1024]{1,0:T(8,128)S(1)}, bf16[16,1024]{1,0:T(8,128)(2,1)S(1)}) custom-call(f32[8,1024]{1,0:T(8,128)S(1)} %copy-done.2, bf16[8,640]{1,0:T(8,128)(2,1)S(1)} %get-tuple-element.55.fresh_ref, bf16[8,640]{1,0:T(8,128)(2,1)S(1)} %collective-permute-done.9.moved_ref, bf16[512,1024]{1,0:T(8,128)(2,1)S(1)} %get-tuple-element.56.weight_ref, ...), custom_call_target="tpu_custom_call" | custom-call | tf_op jit(solution)/shard_map/merge/pallas_call | solution.py:586
  28.0 0.0 copy-start
  28.0 0.0 copy-start.5
  28.0 1.4 %collective-permute-start.13 = (bf16[16,1024]{1,0:T(8,128)(2,1)S(1)}, bf16[16,1024]{1,0:T(8,128)(2,1)S(1)}, u32[]{:S(2)}, u32[]{:S(2)}) collective-permute-start(bf16[16,1024]{1,0:T(8,128)(2,1)S(1)} %get-tuple-element.71.after_ref), channel_id=1, source_target_pairs={{0,17},{1,16},{2,19},{3,18},{4,21},{5,20},{6,23},{7,22},{8,25},{9,... | collective-permute-start | bytes 98312 | tf_op jit(solution)/shard_map/ppermute | solution.py:603
  29.4 1.7 %load.3.late_ref = bf16[1280,1024]{1,0:T(8,128)(2,1)S(1)} custom-call(bf16[2048,1024]{1,0:T(8,128)(2,1)} %source.3, bf16[16,1024]{1,0:T(8,128)(2,1)S(1)} %get-tuple-element.71.after_ref), custom_call_target="tpu_custom_call" | custom-call | bytes 4194304 | tf_op jit(solution)/shard_map/load/pallas_call | solution.py:567
  31.1 0.3 collective-permute-done.13.other_ref
  31.4 0.0 copy-done
  31.4 0.0 copy-done.5
  31.4 1.3 %mlp.1 = (f32[8,512]{1,0:T(8,128)S(1)}, f32[8,512]{1,0:T(8,128)S(1)}) custom-call(f32[8,1024]{1,0:T(8,128)S(1)} %get-tuple-element.70.own_ref, bf16[16,1024]{1,0:T(8,128)(2,1)S(1)} %collective-permute-done.13.other_ref, f32[1,1024]{1,0:T(1,128)S(1)} %bitcast.10, bf16[1024,2048]{1,0:T(8,128)(2,1)S(1)} %copy-done, bf16[768,1024]{1,0:T(8,128)(2,1)S(1)} %load.2.down_ref, ...), custom_call_target="tpu_custom_call" | custom-call | tf_op jit(solution)/shard_map/mlp/pallas_call | solution.py:609
  32.7 1.5 %collective-permute-start.15 = (f32[8,512]{1,0:T(8,128)S(1)}, f32[8,512]{1,0:T(8,128)S(1)}, u32[]{:S(2)}, u32[]{:S(2)}) collective-permute-start(f32[8,512]{1,0:T(8,128)S(1)} %get-tuple-element.74), channel_id=1, source_target_pairs={{0,16},{1,17},{2,18},{3,19},{4,20},{5,21},{6,22},{7,23},{8,24},{9,... | collective-permute-start | bytes 49160 | tf_op jit(solution)/shard_map/ppermute | solution.py:620
  34.2 0.0 collective-permute-start.14
  34.2 1.6 %collective-permute-done.15 = f32[8,512]{1,0:T(8,128)S(1)} collective-permute-done((f32[8,512]{1,0:T(8,128)S(1)}, f32[8,512]{1,0:T(8,128)S(1)}, u32[]{:S(2)}, u32[]{:S(2)}) %collective-permute-start.15) | collective-permute-done | bytes 16416 | tf_op jit(solution)/shard_map/ppermute | solution.py:620
  35.9 0.0 collective-permute-done.14
  35.9 0.6 %select_add_fusion = f32[8,512]{1,0:T(8,128)} fusion(f32[8,512]{1,0:T(8,128)S(1)} %collective-permute-done.15, f32[8,512]{1,0:T(8,128)S(1)} %get-tuple-element.73, f32[8,512]{1,0:T(8,128)S(1)} %collective-permute-done.14, pred[]{:T(512)S(6)} %eq.3), kind=kLoop, calls=%fused_computation.1 | loop fusion | flops 8192 | bytes 65537 | tf_op jit(solution)/shard_map/add | solution.py:626
  (1 shorter events, 0.0 us)
Async XLA Ops:
  0.0 6.9 %copy-start.6 = (s32[24]{0:T(128)S(1)}, s32[24]{0:T(128)}, u32[]{:S(2)}) copy-start(s32[24]{0:T(128)} %param.26) | copy-start | bytes 292
  1.4 6.9 %collective-permute-start.2 = (bf16[8,512]{1,0:T(8,128)(2,1)S(1)}, bf16[8,512]{1,0:T(8,128)(2,1)S(1)}, u32[]{:S(2)}, u32[]{:S(2)}) collective-permute-start(bf16[8,512]{1,0:T(8,128)(2,1)S(1)} %query.1.query_ref), channel_id=1, source_target_pairs={{0,13},{1,12},{2,15},{3,14},{4,9},{5,8},{6,11},{7,10},{8,5},{9,4},... | collective-permute-start | bytes 24584 | tf_op jit(solution)/shard_map/ppermute | solution.py:465
  6.0 4.0 %collective-permute-start.1 = (bf16[8,512]{1,0:T(8,128)(2,1)S(1)}, bf16[8,512]{1,0:T(8,128)(2,1)S(1)}, u32[]{:S(2)}, u32[]{:S(2)}) collective-permute-start(bf16[8,512]{1,0:T(8,128)(2,1)S(1)} %query.1.query_ref), channel_id=1, source_target_pairs={{0,9},{1,8},{2,11},{3,10},{4,13},{5,12},{6,15},{7,14},{8,1},{9,0},... | collective-permute-start | bytes 24584 | tf_op jit(solution)/shard_map/ppermute | solution.py:465
  6.0 4.0 %collective-permute-start = (bf16[8,512]{1,0:T(8,128)(2,1)S(1)}, bf16[8,512]{1,0:T(8,128)(2,1)S(1)}, u32[]{:S(2)}, u32[]{:S(2)}) collective-permute-start(bf16[8,512]{1,0:T(8,128)(2,1)S(1)} %query.1.query_ref), channel_id=1, source_target_pairs={{0,5},{1,4},{2,7},{3,6},{4,1},{5,0},{6,3},{7,2},{8,13},{9,12},{10,... | collective-permute-start | bytes 24584 | tf_op jit(solution)/shard_map/ppermute | solution.py:465
  6.9 7.9 %copy-start.1 = (bf16[24,128,512]{2,1,0:T(8,128)(2,1)S(1)}, bf16[24,128,512]{2,1,0:T(8,128)(2,1)}, u32[]{:S(2)}) copy-start(bf16[24,128,512]{2,1,0:T(8,128)(2,1)} %refs_11_.1) | copy-start | bytes 9437188
  10.0 3.9 %collective-permute-start.3 = (bf16[32,512]{1,0:T(8,128)(2,1)S(1)}, bf16[32,512]{1,0:T(8,128)(2,1)S(1)}, u32[]{:S(2)}, u32[]{:S(2)}) collective-permute-start(bf16[32,512]{1,0:T(8,128)(2,1)S(1)} %pad_maximum_fusion.after_ref.refs_0_), channel_id=1, source_target_pairs={{0,2},{1,3},{2,0},{3,1},{4,6},{5,7},{6,4},{7,5},{8,10},{9,11},{10,... | collective-permute-start | bytes 98312 | tf_op jit(solution)/shard_map/ppermute | solution.py:489
  11.5 3.3 %collective-permute-start.4 = (bf16[32,512]{1,0:T(8,128)(2,1)S(1)}, bf16[32,512]{1,0:T(8,128)(2,1)S(1)}, u32[]{:S(2)}, u32[]{:S(2)}) collective-permute-start(bf16[32,512]{1,0:T(8,128)(2,1)S(1)} %pad_maximum_fusion.after_ref.refs_0_), channel_id=1, source_target_pairs={{0,3},{1,2},{2,1},{3,0},{4,7},{5,6},{6,5},{7,4},{8,11},{9,10},{10,... | collective-permute-start | bytes 98312 | tf_op jit(solution)/shard_map/ppermute | solution.py:489
  12.0 2.9 %collective-permute-start.5 = (bf16[32,512]{1,0:T(8,128)(2,1)S(1)}, bf16[32,512]{1,0:T(8,128)(2,1)S(1)}, u32[]{:S(2)}, u32[]{:S(2)}) collective-permute-start(bf16[32,512]{1,0:T(8,128)(2,1)S(1)} %pad_maximum_fusion.after_ref.refs_0_), channel_id=1, source_target_pairs={{0,1},{1,0},{2,3},{3,2},{4,5},{5,4},{6,7},{7,6},{8,9},{9,8},{10,11... | collective-permute-start | bytes 98312 | tf_op jit(solution)/shard_map/ppermute | solution.py:489
  14.9 4.0 %copy-start.2 = (f32[8,1024]{1,0:T(8,128)S(1)}, f32[8,1024]{1,0:T(8,128)}, u32[]{:S(2)}) copy-start(f32[8,1024]{1,0:T(8,128)} %hidden_ref.3) | copy-start | bytes 98308
  14.9 4.0 %copy-start.3 = (f32[1024]{0:T(1024)S(1)}, f32[1024]{0:T(1024)}, u32[]{:S(2)}) copy-start(f32[1024]{0:T(1024)} %param.15) | copy-start | bytes 12292
  14.9 4.0 %copy-start.4 = (f32[32,8]{0,1:T(8,128)S(1)}, f32[32,8]{0,1:T(8,128)}, u32[]{:S(2)}) copy-start(f32[32,8]{0,1:T(8,128)} %param.21) | copy-start | bytes 3076
  16.7 4.4 %collective-permute-start.6 = (bf16[144,128]{1,0:T(8,128)(2,1)S(1)}, bf16[144,128]{1,0:T(8,128)(2,1)S(1)}, u32[]{:S(2)}, u32[]{:S(2)}) collective-permute-start(bf16[144,128]{1,0:T(8,128)(2,1)S(1)} %get-tuple-element.51), channel_id=1, source_target_pairs={{0,2},{1,3},{2,0},{3,1},{4,6},{5,7},{6,4},{7,5},{8,10},{9,11},{10,... | collective-permute-start | bytes 110600 | tf_op jit(solution)/shard_map/ppermute | solution.py:527
  17.7 3.7 %collective-permute-start.7 = (bf16[144,128]{1,0:T(8,128)(2,1)S(1)}, bf16[144,128]{1,0:T(8,128)(2,1)S(1)}, u32[]{:S(2)}, u32[]{:S(2)}) collective-permute-start(bf16[144,128]{1,0:T(8,128)(2,1)S(1)} %get-tuple-element.52), channel_id=1, source_target_pairs={{0,3},{1,2},{2,1},{3,0},{4,7},{5,6},{6,5},{7,4},{8,11},{9,10},{10,... | collective-permute-start | bytes 110600 | tf_op jit(solution)/shard_map/ppermute | solution.py:527
  18.4 2.9 %collective-permute-start.8 = (bf16[144,128]{1,0:T(8,128)(2,1)S(1)}, bf16[144,128]{1,0:T(8,128)(2,1)S(1)}, u32[]{:S(2)}, u32[]{:S(2)}) collective-permute-start(bf16[144,128]{1,0:T(8,128)(2,1)S(1)} %get-tuple-element.53), channel_id=1, source_target_pairs={{0,1},{1,0},{2,3},{3,2},{4,5},{5,4},{6,7},{7,6},{8,9},{9,8},{10,11... | collective-permute-start | bytes 110600 | tf_op jit(solution)/shard_map/ppermute | solution.py:527
  21.7 5.7 %collective-permute-start.10 = (bf16[8,640]{1,0:T(8,128)(2,1)S(1)}, bf16[8,640]{1,0:T(8,128)(2,1)S(1)}, u32[]{:S(2)}, u32[]{:S(2)}) collective-permute-start(bf16[8,640]{1,0:T(8,128)(2,1)S(1)} %get-tuple-element.63), channel_id=1, source_target_pairs={{0,13},{1,12},{2,15},{3,14},{4,9},{5,8},{6,11},{7,10},{8,5},{9,4},... | collective-permute-start | bytes 30728 | tf_op jit(solution)/shard_map/ppermute | solution.py:580
  23.3 4.2 %collective-permute-start.11 = (bf16[8,640]{1,0:T(8,128)(2,1)S(1)}, bf16[8,640]{1,0:T(8,128)(2,1)S(1)}, u32[]{:S(2)}, u32[]{:S(2)}) collective-permute-start(bf16[8,640]{1,0:T(8,128)(2,1)S(1)} %get-tuple-element.64), channel_id=1, source_target_pairs={{0,9},{1,8},{2,11},{3,10},{4,13},{5,12},{6,15},{7,14},{8,1},{9,0},... | collective-permute-start | bytes 30728 | tf_op jit(solution)/shard_map/ppermute | solution.py:580
  24.1 3.4 %collective-permute-start.12 = (bf16[8,640]{1,0:T(8,128)(2,1)S(1)}, bf16[8,640]{1,0:T(8,128)(2,1)S(1)}, u32[]{:S(2)}, u32[]{:S(2)}) collective-permute-start(bf16[8,640]{1,0:T(8,128)(2,1)S(1)} %get-tuple-element.65), channel_id=1, source_target_pairs={{0,5},{1,4},{2,7},{3,6},{4,1},{5,0},{6,3},{7,2},{8,13},{9,12},{10,... | collective-permute-start | bytes 30728 | tf_op jit(solution)/shard_map/ppermute | solution.py:580
  25.6 1.9 %collective-permute-start.9 = (bf16[8,640]{1,0:T(8,128)(2,1)S(1)}, bf16[8,640]{1,0:T(8,128)(2,1)S(1)}, u32[]{:S(2)}, u32[]{:S(2)}) collective-permute-start(bf16[8,640]{1,0:T(8,128)(2,1)S(1)} %get-tuple-element.55.fresh_ref), channel_id=1, source_target_pairs={{0,1},{1,0},{2,3},{3,2},{4,5},{5,4},{6,7},{7,6},{8,9},{9,8},{10,11... | collective-permute-start | bytes 30728 | tf_op jit(solution)/shard_map/ppermute | solution.py:584
  28.0 3.4 %copy-start = (bf16[1024,2048]{1,0:T(8,128)(2,1)S(1)}, bf16[1024,2048]{1,0:T(8,128)(2,1)}, u32[]{:S(2)}) copy-start(bf16[1024,2048]{1,0:T(8,128)(2,1)} %up_ref.1) | copy-start | bytes 12582916
  28.0 3.4 %copy-start.5 = (f32[1024]{0:T(1024)S(1)}, f32[1024]{0:T(1024)}, u32[]{:S(2)}) copy-start(f32[1024]{0:T(1024)} %param.16) | copy-start | bytes 12292
  28.0 3.4 %collective-permute-start.13 = (bf16[16,1024]{1,0:T(8,128)(2,1)S(1)}, bf16[16,1024]{1,0:T(8,128)(2,1)S(1)}, u32[]{:S(2)}, u32[]{:S(2)}) collective-permute-start(bf16[16,1024]{1,0:T(8,128)(2,1)S(1)} %get-tuple-element.71.after_ref), channel_id=1, source_target_pairs={{0,17},{1,16},{2,19},{3,18},{4,21},{5,20},{6,23},{7,22},{8,25},{9,... | collective-permute-start | bytes 98312 | tf_op jit(solution)/shard_map/ppermute | solution.py:603
  32.7 3.2 %collective-permute-start.15 = (f32[8,512]{1,0:T(8,128)S(1)}, f32[8,512]{1,0:T(8,128)S(1)}, u32[]{:S(2)}, u32[]{:S(2)}) collective-permute-start(f32[8,512]{1,0:T(8,128)S(1)} %get-tuple-element.74), channel_id=1, source_target_pairs={{0,16},{1,17},{2,18},{3,19},{4,20},{5,21},{6,22},{7,23},{8,24},{9,... | collective-permute-start | bytes 49160 | tf_op jit(solution)/shard_map/ppermute | solution.py:620
  34.2 1.6 %collective-permute-start.14 = (f32[8,512]{1,0:T(8,128)S(1)}, f32[8,512]{1,0:T(8,128)S(1)}, u32[]{:S(2)}, u32[]{:S(2)}) collective-permute-start(f32[8,512]{1,0:T(8,128)S(1)} %get-tuple-element.73), channel_id=1, source_target_pairs={{0,1},{1,0},{2,3},{3,2},{4,5},{5,4},{6,7},{7,6},{8,9},{9,8},{10,11... | collective-permute-start | bytes 49160 | tf_op jit(solution)/shard_map/ppermute | solution.py:621
where the time goes:
time: 36.7 us; the launch traced here: 36.5 us
  starting transfers between devices  17 us (46%)
  Pallas kernels  13.7 us (37%)
  waiting for transfers between devices  4.99 us (14%)
  other arithmetic  0.61 us (2%)
    ppermute x3, starting transfers between devices, per_device(): lax.ppermute(query, 'blk', xor_pairs(blocks, step * inner ^ 1))  5.48 us
    ppermute x3, starting transfers between devices, per_device(): lax.ppermute(sums[step], 'blk', xor_pairs(blocks, step * inner ^ 1))  3.89 us
    pallas_call x2, Pallas kernels, load_down(): pl.pallas_call(functools.partial(load_kernel, start), out_shape=pltpu.VME...  3.1 us
    pallas_call x1, Pallas kernels, per_device(): pl.pallas_call(side_kernel, out_shape=(shape((own_rows, width + LANES), b...  2.17 us
    ppermute x3, starting transfers between devices, per_device(): lax.ppermute(sums[i], 'blk', xor_pairs(blocks, steps[i]))  2.17 us
    ppermute x3, starting transfers between devices, per_device(): lax.ppermute(near, 'blk', xor_pairs(blocks, step))  2.14 us
    pallas_call x1, Pallas kernels, per_device(): pl.pallas_call(functools.partial(attend_kernel, groups), out_shape=(shape...  1.78 us
    ppermute x3, waiting for transfers between devices, per_device(): lax.ppermute(query, 'blk', xor_pairs(blocks, step * inner ^ 1))  1.7 us
  transfers between devices with their start and end apart: 16, of which 6 were waited for; matrix products, arithmetic and copies ran while one was open for 0% of the time, Pallas kernels for 23%

commit v1 on v0

--- a/solution.py
+++ b/solution.py
@@ -285,7 +285,9 @@
         weights = jnp.concatenate(blocks, axis=0).astype(jnp.bfloat16)
         block = values_ref[c * chunk : (c + 1) * chunk]
         mixes.append(dot(weights, block.reshape(chunk * PAGE, width)))
-    totals = [jnp.sum(weight, axis=1, keepdims=True) for weight in page_weights]
+    ones = jnp.ones((2 * PAGE, LANES), jnp.bfloat16)
+    totals = pieces(jnp.concatenate(page_weights, axis=0), 2)
+    totals = dot(jnp.concatenate(totals, axis=1), ones)
     tops = jnp.zeros((PIECE, LANES), jnp.float32)
     for p in range(page_count):
         tops = jnp.where(lane == p, page_tops[p], tops)
@@ -295,7 +297,8 @@
         for p in range(c * chunk, (c + 1) * chunk):
             peak = jnp.max(tops + apart_ref[p : p + 1], axis=1, keepdims=True)
             factor = jnp.exp(page_tops[p] - peak)
-            total = jnp.where(lane == row + SUM_LANE, totals[p] * factor, 0.0)
+            total = totals[p * PIECE : (p + 1) * PIECE] * factor
+            total = jnp.where(lane == row + SUM_LANE, total, 0.0)
             stats.append(jnp.where(lane == row, peak * lead_ref[p : p + 1], total))
             factors.append(factor)
         mixes[c] = mixes[c] * (pair_heads * jnp.concatenate(factors, axis=0))

time: 36.7 us -> 36.7 us (level)
  no operation moved by 1% of the time
where the time goes in v1:
time: 36.7 us; the launch traced here: 36.5 us
  starting transfers between devices  17 us (46%)
  Pallas kernels  13.7 us (37%)
  waiting for transfers between devices  4.99 us (14%)
  other arithmetic  0.61 us (2%)
    ppermute x3, starting transfers between devices, per_device(): lax.ppermute(query, 'blk', xor_pairs(blocks, step * inner ^ 1))  5.48 us
    ppermute x3, starting transfers between devices, per_device(): lax.ppermute(sums[step], 'blk', xor_pairs(blocks, step * inner ^ 1))  3.89 us
    pallas_call x2, Pallas kernels, load_down(): pl.pallas_call(functools.partial(load_kernel, start), out_shape=pltpu.VME...  3.1 us
    pallas_call x1, Pallas kernels, per_device(): pl.pallas_call(side_kernel, out_shape=(shape((own_rows, width + LANES), b...  2.17 us
    ppermute x3, starting transfers between devices, per_device(): lax.ppermute(sums[i], 'blk', xor_pairs(blocks, steps[i]))  2.15 us
    ppermute x3, starting transfers between devices, per_device(): lax.ppermute(near, 'blk', xor_pairs(blocks, step))  2.14 us
    pallas_call x1, Pallas kernels, per_device(): pl.pallas_call(functools.partial(attend_kernel, groups), out_shape=(shape...  1.82 us
    ppermute x3, waiting for transfers between devices, per_device(): lax.ppermute(query, 'blk', xor_pairs(blocks, step * inner ^ 1))  1.7 us
  transfers between devices with their start and end apart: 16, of which 6 were waited for; matrix products, arithmetic and copies ran while one was open for 0% of the time, Pallas kernels for 23%

profile of v1, /device:TPU:0, one launch (start us, length us, event | category | flops | bytes accessed | tf_op | source)
XLA Modules:
  0.0 36.5 jit_solution(14585074668468116128)
XLA Ops:
  0.0 0.0 copy-start.6
  0.0 1.4 %query.1.query_ref = bf16[8,512]{1,0:T(8,128)(2,1)S(1)} custom-call(f32[8,1024]{1,0:T(8,128)} %hidden_ref.3, f32[1,1024]{1,0:T(1,128)} %bitcast.6, bf16[3,1024,512]{2,1,0:T(8,128)(2,1)} %weight_hbm.3), custom_call_target="tpu_custom_call" | custom-call | tf_op jit(solution)/shard_map/query/pallas_call | solution.py:449
  1.4 4.6 %collective-permute-start.2 = (bf16[8,512]{1,0:T(8,128)(2,1)S(1)}, bf16[8,512]{1,0:T(8,128)(2,1)S(1)}, u32[]{:S(2)}, u32[]{:S(2)}) collective-permute-start(bf16[8,512]{1,0:T(8,128)(2,1)S(1)} %query.1.query_ref), channel_id=1, source_target_pairs={{0,13},{1,12},{2,15},{3,14},{4,9},{5,8},{6,11},{7,10},{8,5},{9,4},... | collective-permute-start | bytes 24584 | tf_op jit(solution)/shard_map/ppermute | solution.py:468
  6.0 0.0 collective-permute-start.1
  6.0 0.9 %collective-permute-start = (bf16[8,512]{1,0:T(8,128)(2,1)S(1)}, bf16[8,512]{1,0:T(8,128)(2,1)S(1)}, u32[]{:S(2)}, u32[]{:S(2)}) collective-permute-start(bf16[8,512]{1,0:T(8,128)(2,1)S(1)} %query.1.query_ref), channel_id=1, source_target_pairs={{0,5},{1,4},{2,7},{3,6},{4,1},{5,0},{6,3},{7,2},{8,13},{9,12},{10,... | collective-permute-start | bytes 24584 | tf_op jit(solution)/shard_map/ppermute | solution.py:468
  6.9 0.0 copy-done.6
  6.9 0.0 copy-start.1
  6.9 1.4 %pages.1 = (bf16[8,128,512]{2,1,0:T(8,128)(2,1)S(1)}, bf16[192,128]{1,0:T(8,128)(2,1)S(1)}, bf16[128,192]{1,0:T(8,128)(2,1)S(1)}, f32[24,128]{1,0:T(8,128)S(1)},...) custom-call(bf16[8,512]{1,0:T(8,128)(2,1)S(1)} %query.1.query_ref, s32[1,24]{1,0:T(1,128)S(1)} %bitcast.11, ...), custom_call_target="tpu_custom_call" | custom-call | bytes 3145728 | tf_op jit(solution)/shard_map/pages/pallas_call | solution.py:473
  8.3 0.0 collective-permute-done.2
  8.3 1.7 %collective-permute-done.1 = bf16[8,512]{1,0:T(8,128)(2,1)S(1)} collective-permute-done((bf16[8,512]{1,0:T(8,128)(2,1)S(1)}, bf16[8,512]{1,0:T(8,128)(2,1)S(1)}, u32[]{:S(2)}, u32[]{:S(2)}) %collective-permute-start.1) | collective-permute-done | bytes 8224 | tf_op jit(solution)/shard_map/ppermute | solution.py:468
  10.0 0.0 collective-permute-done
  10.0 1.5 %collective-permute-start.3 = (bf16[32,512]{1,0:T(8,128)(2,1)S(1)}, bf16[32,512]{1,0:T(8,128)(2,1)S(1)}, u32[]{:S(2)}, u32[]{:S(2)}) collective-permute-start(bf16[32,512]{1,0:T(8,128)(2,1)S(1)} %pad_maximum_fusion.after_ref.refs_0_), channel_id=1, source_target_pairs={{0,2},{1,3},{2,0},{3,1},{4,6},{5,7},{6,4},{7,5},{8,10},{9,11},{10,... | collective-permute-start | bytes 98312 | tf_op jit(solution)/shard_map/ppermute | solution.py:492
  11.5 0.5 %collective-permute-start.4 = (bf16[32,512]{1,0:T(8,128)(2,1)S(1)}, bf16[32,512]{1,0:T(8,128)(2,1)S(1)}, u32[]{:S(2)}, u32[]{:S(2)}) collective-permute-start(bf16[32,512]{1,0:T(8,128)(2,1)S(1)} %pad_maximum_fusion.after_ref.refs_0_), channel_id=1, source_target_pairs={{0,3},{1,2},{2,1},{3,0},{4,7},{5,6},{6,5},{7,4},{8,11},{9,10},{10,... | collective-permute-start | bytes 98312 | tf_op jit(solution)/shard_map/ppermute | solution.py:492
  12.0 0.2 collective-permute-start.5
  12.2 1.6 %bias.1 = (bf16[16,128,512]{2,1,0:T(8,128)(2,1)S(1)}, f32[192,128]{1,0:T(8,128)S(1)}) custom-call(f32[8,32]{1,0:T(8,128)} %bitcast.8, s32[31]{0:T(128)} %edges_hbm.1, s32[1,128]{1,0:T(1,128)} %bitcast.12, s32[1,24]{1,0:T(1,128)} %bitcast.13, s32[24,128]{1,0:T(8,128)S(1)} %get-tuple-element.42.owners_ref, bf16[24,128,512]{2,1,0:T(8,128)(2,1)} %keys_hbm.3, ...), custom_call_target="tpu_custom_call" | custom-call | bytes 3145728 | tf_op jit(solution)/shard_map/bias/pallas_call | solution.py:494
  13.8 0.2 collective-permute-done.3.refs_1_
  14.0 0.9 %collective-permute-done.4.refs_2_ = bf16[32,512]{1,0:T(8,128)(2,1)S(1)} collective-permute-done((bf16[32,512]{1,0:T(8,128)(2,1)S(1)}, bf16[32,512]{1,0:T(8,128)(2,1)S(1)}, u32[]{:S(2)}, u32[]{:S(2)}) %collective-permute-start.4) | collective-permute-done | bytes 32800 | tf_op jit(solution)/shard_map/ppermute | solution.py:492
  14.9 0.0 collective-permute-done.5.refs_3_
  14.9 0.0 copy-done.1
  14.9 0.0 copy-start.2
  14.9 0.0 copy-start.3
  14.9 0.0 copy-start.4
  14.9 1.8 %attend.1 = (bf16[144,128]{1,0:T(8,128)(2,1)S(1)}, bf16[144,128]{1,0:T(8,128)(2,1)S(1)}, bf16[144,128]{1,0:T(8,128)(2,1)S(1)}, bf16[144,128]{1,0:T(8,128)(2,1)S(1)}) custom-call(bf16[32,512]{1,0:T(8,128)(2,1)S(1)} %pad_maximum_fusion.after_ref.refs_0_, bf16[32,512]{1,0:T(8,128)(2,1)S(1)} %collective-permute-done.3.refs_1_, ...), custom_call_target="tpu_custom_call" | custom-call | tf_op jit(solution)/shard_map/attend/pallas_call | solution.py:521
  16.7 1.0 %collective-permute-start.6 = (bf16[144,128]{1,0:T(8,128)(2,1)S(1)}, bf16[144,128]{1,0:T(8,128)(2,1)S(1)}, u32[]{:S(2)}, u32[]{:S(2)}) collective-permute-start(bf16[144,128]{1,0:T(8,128)(2,1)S(1)} %get-tuple-element.51), channel_id=1, source_target_pairs={{0,2},{1,3},{2,0},{3,1},{4,6},{5,7},{6,4},{7,5},{8,10},{9,11},{10,... | collective-permute-start | bytes 110600 | tf_op jit(solution)/shard_map/ppermute | solution.py:530
  17.7 0.8 %collective-permute-start.7 = (bf16[144,128]{1,0:T(8,128)(2,1)S(1)}, bf16[144,128]{1,0:T(8,128)(2,1)S(1)}, u32[]{:S(2)}, u32[]{:S(2)}) collective-permute-start(bf16[144,128]{1,0:T(8,128)(2,1)S(1)} %get-tuple-element.52), channel_id=1, source_target_pairs={{0,3},{1,2},{2,1},{3,0},{4,7},{5,6},{6,5},{7,4},{8,11},{9,10},{10,... | collective-permute-start | bytes 110600 | tf_op jit(solution)/shard_map/ppermute | solution.py:530
  18.4 0.4 %collective-permute-start.8 = (bf16[144,128]{1,0:T(8,128)(2,1)S(1)}, bf16[144,128]{1,0:T(8,128)(2,1)S(1)}, u32[]{:S(2)}, u32[]{:S(2)}) collective-permute-start(bf16[144,128]{1,0:T(8,128)(2,1)S(1)} %get-tuple-element.53), channel_id=1, source_target_pairs={{0,1},{1,0},{2,3},{3,2},{4,5},{5,4},{6,7},{7,6},{8,9},{9,8},{10,11... | collective-permute-start | bytes 110600 | tf_op jit(solution)/shard_map/ppermute | solution.py:530
  18.9 0.0 copy-done.2
  18.9 0.0 copy-done.3
  18.9 0.0 copy-done.4
  18.9 2.2 %side.1 = (bf16[8,640]{1,0:T(8,128)(2,1)S(1)}, bf16[512,1024]{1,0:T(8,128)(2,1)S(1)}, bf16[256,512]{1,0:T(8,128)(2,1)S(1)}) custom-call(f32[8,1024]{1,0:T(8,128)S(1)} %copy-done.2, f32[1,1024]{1,0:T(1,128)S(1)} %bitcast.7, bf16[8,512]{1,0:T(8,128)(2,1)S(1)} %query.1.query_ref, f32[8,32]{1,0:T(8,128)S(1)} %bitcast.9, bf16[3,1024,512]{2,1,0:T(8,128)(2,1)} %weight_hbm.3, ...), custom_call_target="tpu_custom_call" | custom-call | bytes 3145728 | tf_op jit(solution)/shard_map/side/pallas_call | solution.py:534
  21.1 0.0 collective-permute-done.6.refs_1_
  21.1 0.3 collective-permute-done.7.refs_2_
  21.4 0.0 collective-permute-done.8.refs_3_
  21.4 0.4 %combine.1 = (bf16[8,640]{1,0:T(8,128)(2,1)S(1)}, bf16[8,640]{1,0:T(8,128)(2,1)S(1)}, bf16[8,640]{1,0:T(8,128)(2,1)S(1)}, bf16[8,640]{1,0:T(8,128)(2,1)S(1)}) custom-call(bf16[144,128]{1,0:T(8,128)(2,1)S(1)} %get-tuple-element.58.after_ref.refs_0_, bf16[144,128]{1,0:T(8,128)(2,1)S(1)} %collective-permute-done.6.refs_1_, ...), custom_call_target="tpu_custom_call" | custom-call | tf_op jit(solution)/shard_map/combine/pallas_call | solution.py:558
  21.8 1.5 %collective-permute-start.10 = (bf16[8,640]{1,0:T(8,128)(2,1)S(1)}, bf16[8,640]{1,0:T(8,128)(2,1)S(1)}, u32[]{:S(2)}, u32[]{:S(2)}) collective-permute-start(bf16[8,640]{1,0:T(8,128)(2,1)S(1)} %get-tuple-element.63), channel_id=1, source_target_pairs={{0,13},{1,12},{2,15},{3,14},{4,9},{5,8},{6,11},{7,10},{8,5},{9,4},... | collective-permute-start | bytes 30728 | tf_op jit(solution)/shard_map/ppermute | solution.py:583
  23.3 0.8 %collective-permute-start.11 = (bf16[8,640]{1,0:T(8,128)(2,1)S(1)}, bf16[8,640]{1,0:T(8,128)(2,1)S(1)}, u32[]{:S(2)}, u32[]{:S(2)}) collective-permute-start(bf16[8,640]{1,0:T(8,128)(2,1)S(1)} %get-tuple-element.64), channel_id=1, source_target_pairs={{0,9},{1,8},{2,11},{3,10},{4,13},{5,12},{6,15},{7,14},{8,1},{9,0},... | collective-permute-start | bytes 30728 | tf_op jit(solution)/shard_map/ppermute | solution.py:583
  24.1 1.5 %collective-permute-start.12 = (bf16[8,640]{1,0:T(8,128)(2,1)S(1)}, bf16[8,640]{1,0:T(8,128)(2,1)S(1)}, u32[]{:S(2)}, u32[]{:S(2)}) collective-permute-start(bf16[8,640]{1,0:T(8,128)(2,1)S(1)} %get-tuple-element.65), channel_id=1, source_target_pairs={{0,5},{1,4},{2,7},{3,6},{4,1},{5,0},{6,3},{7,2},{8,13},{9,12},{10,... | collective-permute-start | bytes 30728 | tf_op jit(solution)/shard_map/ppermute | solution.py:583
  25.6 0.4 %collective-permute-start.9 = (bf16[8,640]{1,0:T(8,128)(2,1)S(1)}, bf16[8,640]{1,0:T(8,128)(2,1)S(1)}, u32[]{:S(2)}, u32[]{:S(2)}) collective-permute-start(bf16[8,640]{1,0:T(8,128)(2,1)S(1)} %get-tuple-element.55.fresh_ref), channel_id=1, source_target_pairs={{0,1},{1,0},{2,3},{3,2},{4,5},{5,4},{6,7},{7,6},{8,9},{9,8},{10,11... | collective-permute-start | bytes 30728 | tf_op jit(solution)/shard_map/ppermute | solution.py:587
  26.1 1.4 %load.2.down_ref = bf16[768,1024]{1,0:T(8,128)(2,1)S(1)} custom-call(bf16[2048,1024]{1,0:T(8,128)(2,1)} %source.3, bf16[8,640]{1,0:T(8,128)(2,1)S(1)} %get-tuple-element.66.after_ref.refs_0_), custom_call_target="tpu_custom_call" | custom-call | bytes 4194304 | tf_op jit(solution)/shard_map/load/pallas_call | solution.py:570
  27.5 0.0 collective-permute-done.10.refs_1_
  27.5 0.0 collective-permute-done.11.refs_2_
  27.5 0.0 collective-permute-done.12.refs_3_
  27.5 0.0 collective-permute-done.9.moved_ref
  27.5 0.5 %merge.1 = (f32[8,1024]{1,0:T(8,128)S(1)}, bf16[16,1024]{1,0:T(8,128)(2,1)S(1)}) custom-call(f32[8,1024]{1,0:T(8,128)S(1)} %copy-done.2, bf16[8,640]{1,0:T(8,128)(2,1)S(1)} %get-tuple-element.55.fresh_ref, bf16[8,640]{1,0:T(8,128)(2,1)S(1)} %collective-permute-done.9.moved_ref, bf16[512,1024]{1,0:T(8,128)(2,1)S(1)} %get-tuple-element.56.weight_ref, ...), custom_call_target="tpu_custom_call" | custom-call | tf_op jit(solution)/shard_map/merge/pallas_call | solution.py:589
  28.0 0.0 copy-start
  28.0 0.0 copy-start.5
  28.0 1.4 %collective-permute-start.13 = (bf16[16,1024]{1,0:T(8,128)(2,1)S(1)}, bf16[16,1024]{1,0:T(8,128)(2,1)S(1)}, u32[]{:S(2)}, u32[]{:S(2)}) collective-permute-start(bf16[16,1024]{1,0:T(8,128)(2,1)S(1)} %get-tuple-element.71.after_ref), channel_id=1, source_target_pairs={{0,17},{1,16},{2,19},{3,18},{4,21},{5,20},{6,23},{7,22},{8,25},{9,... | collective-permute-start | bytes 98312 | tf_op jit(solution)/shard_map/ppermute | solution.py:606
  29.4 1.7 %load.3.late_ref = bf16[1280,1024]{1,0:T(8,128)(2,1)S(1)} custom-call(bf16[2048,1024]{1,0:T(8,128)(2,1)} %source.3, bf16[16,1024]{1,0:T(8,128)(2,1)S(1)} %get-tuple-element.71.after_ref), custom_call_target="tpu_custom_call" | custom-call | bytes 4194304 | tf_op jit(solution)/shard_map/load/pallas_call | solution.py:570
  31.2 0.3 collective-permute-done.13.other_ref
  31.5 0.0 copy-done
  31.5 0.0 copy-done.5
  31.5 1.3 %mlp.1 = (f32[8,512]{1,0:T(8,128)S(1)}, f32[8,512]{1,0:T(8,128)S(1)}) custom-call(f32[8,1024]{1,0:T(8,128)S(1)} %get-tuple-element.70.own_ref, bf16[16,1024]{1,0:T(8,128)(2,1)S(1)} %collective-permute-done.13.other_ref, f32[1,1024]{1,0:T(1,128)S(1)} %bitcast.10, bf16[1024,2048]{1,0:T(8,128)(2,1)S(1)} %copy-done, bf16[768,1024]{1,0:T(8,128)(2,1)S(1)} %load.2.down_ref, ...), custom_call_target="tpu_custom_call" | custom-call | tf_op jit(solution)/shard_map/mlp/pallas_call | solution.py:612
  32.7 1.5 %collective-permute-start.15 = (f32[8,512]{1,0:T(8,128)S(1)}, f32[8,512]{1,0:T(8,128)S(1)}, u32[]{:S(2)}, u32[]{:S(2)}) collective-permute-start(f32[8,512]{1,0:T(8,128)S(1)} %get-tuple-element.74), channel_id=1, source_target_pairs={{0,16},{1,17},{2,18},{3,19},{4,20},{5,21},{6,22},{7,23},{8,24},{9,... | collective-permute-start | bytes 49160 | tf_op jit(solution)/shard_map/ppermute | solution.py:623
  34.3 0.0 collective-permute-start.14
  34.3 1.6 %collective-permute-done.15 = f32[8,512]{1,0:T(8,128)S(1)} collective-permute-done((f32[8,512]{1,0:T(8,128)S(1)}, f32[8,512]{1,0:T(8,128)S(1)}, u32[]{:S(2)}, u32[]{:S(2)}) %collective-permute-start.15) | collective-permute-done | bytes 16416 | tf_op jit(solution)/shard_map/ppermute | solution.py:623
  35.9 0.0 collective-permute-done.14
  35.9 0.6 %select_add_fusion = f32[8,512]{1,0:T(8,128)} fusion(f32[8,512]{1,0:T(8,128)S(1)} %collective-permute-done.15, f32[8,512]{1,0:T(8,128)S(1)} %get-tuple-element.73, f32[8,512]{1,0:T(8,128)S(1)} %collective-permute-done.14, pred[]{:T(512)S(6)} %eq.3), kind=kLoop, calls=%fused_computation.1 | loop fusion | flops 8192 | bytes 65537 | tf_op jit(solution)/shard_map/add | solution.py:629
  (1 shorter events, 0.0 us)
Async XLA Ops:
  0.0 6.9 %copy-start.6 = (s32[24]{0:T(128)S(1)}, s32[24]{0:T(128)}, u32[]{:S(2)}) copy-start(s32[24]{0:T(128)} %param.26) | copy-start | bytes 292
  1.4 6.9 %collective-permute-start.2 = (bf16[8,512]{1,0:T(8,128)(2,1)S(1)}, bf16[8,512]{1,0:T(8,128)(2,1)S(1)}, u32[]{:S(2)}, u32[]{:S(2)}) collective-permute-start(bf16[8,512]{1,0:T(8,128)(2,1)S(1)} %query.1.query_ref), channel_id=1, source_target_pairs={{0,13},{1,12},{2,15},{3,14},{4,9},{5,8},{6,11},{7,10},{8,5},{9,4},... | collective-permute-start | bytes 24584 | tf_op jit(solution)/shard_map/ppermute | solution.py:468
  6.0 4.0 %collective-permute-start.1 = (bf16[8,512]{1,0:T(8,128)(2,1)S(1)}, bf16[8,512]{1,0:T(8,128)(2,1)S(1)}, u32[]{:S(2)}, u32[]{:S(2)}) collective-permute-start(bf16[8,512]{1,0:T(8,128)(2,1)S(1)} %query.1.query_ref), channel_id=1, source_target_pairs={{0,9},{1,8},{2,11},{3,10},{4,13},{5,12},{6,15},{7,14},{8,1},{9,0},... | collective-permute-start | bytes 24584 | tf_op jit(solution)/shard_map/ppermute | solution.py:468
  6.0 4.0 %collective-permute-start = (bf16[8,512]{1,0:T(8,128)(2,1)S(1)}, bf16[8,512]{1,0:T(8,128)(2,1)S(1)}, u32[]{:S(2)}, u32[]{:S(2)}) collective-permute-start(bf16[8,512]{1,0:T(8,128)(2,1)S(1)} %query.1.query_ref), channel_id=1, source_target_pairs={{0,5},{1,4},{2,7},{3,6},{4,1},{5,0},{6,3},{7,2},{8,13},{9,12},{10,... | collective-permute-start | bytes 24584 | tf_op jit(solution)/shard_map/ppermute | solution.py:468
  6.9 7.9 %copy-start.1 = (bf16[24,128,512]{2,1,0:T(8,128)(2,1)S(1)}, bf16[24,128,512]{2,1,0:T(8,128)(2,1)}, u32[]{:S(2)}) copy-start(bf16[24,128,512]{2,1,0:T(8,128)(2,1)} %refs_11_.1) | copy-start | bytes 9437188
  10.0 3.9 %collective-permute-start.3 = (bf16[32,512]{1,0:T(8,128)(2,1)S(1)}, bf16[32,512]{1,0:T(8,128)(2,1)S(1)}, u32[]{:S(2)}, u32[]{:S(2)}) collective-permute-start(bf16[32,512]{1,0:T(8,128)(2,1)S(1)} %pad_maximum_fusion.after_ref.refs_0_), channel_id=1, source_target_pairs={{0,2},{1,3},{2,0},{3,1},{4,6},{5,7},{6,4},{7,5},{8,10},{9,11},{10,... | collective-permute-start | bytes 98312 | tf_op jit(solution)/shard_map/ppermute | solution.py:492
  11.5 3.3 %collective-permute-start.4 = (bf16[32,512]{1,0:T(8,128)(2,1)S(1)}, bf16[32,512]{1,0:T(8,128)(2,1)S(1)}, u32[]{:S(2)}, u32[]{:S(2)}) collective-permute-start(bf16[32,512]{1,0:T(8,128)(2,1)S(1)} %pad_maximum_fusion.after_ref.refs_0_), channel_id=1, source_target_pairs={{0,3},{1,2},{2,1},{3,0},{4,7},{5,6},{6,5},{7,4},{8,11},{9,10},{10,... | collective-permute-start | bytes 98312 | tf_op jit(solution)/shard_map/ppermute | solution.py:492
  12.0 2.9 %collective-permute-start.5 = (bf16[32,512]{1,0:T(8,128)(2,1)S(1)}, bf16[32,512]{1,0:T(8,128)(2,1)S(1)}, u32[]{:S(2)}, u32[]{:S(2)}) collective-permute-start(bf16[32,512]{1,0:T(8,128)(2,1)S(1)} %pad_maximum_fusion.after_ref.refs_0_), channel_id=1, source_target_pairs={{0,1},{1,0},{2,3},{3,2},{4,5},{5,4},{6,7},{7,6},{8,9},{9,8},{10,11... | collective-permute-start | bytes 98312 | tf_op jit(solution)/shard_map/ppermute | solution.py:492
  14.9 4.0 %copy-start.2 = (f32[8,1024]{1,0:T(8,128)S(1)}, f32[8,1024]{1,0:T(8,128)}, u32[]{:S(2)}) copy-start(f32[8,1024]{1,0:T(8,128)} %hidden_ref.3) | copy-start | bytes 98308
  14.9 4.0 %copy-start.3 = (f32[1024]{0:T(1024)S(1)}, f32[1024]{0:T(1024)}, u32[]{:S(2)}) copy-start(f32[1024]{0:T(1024)} %param.15) | copy-start | bytes 12292
  14.9 4.0 %copy-start.4 = (f32[32,8]{0,1:T(8,128)S(1)}, f32[32,8]{0,1:T(8,128)}, u32[]{:S(2)}) copy-start(f32[32,8]{0,1:T(8,128)} %param.21) | copy-start | bytes 3076
  16.7 4.3 %collective-permute-start.6 = (bf16[144,128]{1,0:T(8,128)(2,1)S(1)}, bf16[144,128]{1,0:T(8,128)(2,1)S(1)}, u32[]{:S(2)}, u32[]{:S(2)}) collective-permute-start(bf16[144,128]{1,0:T(8,128)(2,1)S(1)} %get-tuple-element.51), channel_id=1, source_target_pairs={{0,2},{1,3},{2,0},{3,1},{4,6},{5,7},{6,4},{7,5},{8,10},{9,11},{10,... | collective-permute-start | bytes 110600 | tf_op jit(solution)/shard_map/ppermute | solution.py:530
  17.7 3.7 %collective-permute-start.7 = (bf16[144,128]{1,0:T(8,128)(2,1)S(1)}, bf16[144,128]{1,0:T(8,128)(2,1)S(1)}, u32[]{:S(2)}, u32[]{:S(2)}) collective-permute-start(bf16[144,128]{1,0:T(8,128)(2,1)S(1)} %get-tuple-element.52), channel_id=1, source_target_pairs={{0,3},{1,2},{2,1},{3,0},{4,7},{5,6},{6,5},{7,4},{8,11},{9,10},{10,... | collective-permute-start | bytes 110600 | tf_op jit(solution)/shard_map/ppermute | solution.py:530
  18.4 2.9 %collective-permute-start.8 = (bf16[144,128]{1,0:T(8,128)(2,1)S(1)}, bf16[144,128]{1,0:T(8,128)(2,1)S(1)}, u32[]{:S(2)}, u32[]{:S(2)}) collective-permute-start(bf16[144,128]{1,0:T(8,128)(2,1)S(1)} %get-tuple-element.53), channel_id=1, source_target_pairs={{0,1},{1,0},{2,3},{3,2},{4,5},{5,4},{6,7},{7,6},{8,9},{9,8},{10,11... | collective-permute-start | bytes 110600 | tf_op jit(solution)/shard_map/ppermute | solution.py:530
  21.8 5.7 %collective-permute-start.10 = (bf16[8,640]{1,0:T(8,128)(2,1)S(1)}, bf16[8,640]{1,0:T(8,128)(2,1)S(1)}, u32[]{:S(2)}, u32[]{:S(2)}) collective-permute-start(bf16[8,640]{1,0:T(8,128)(2,1)S(1)} %get-tuple-element.63), channel_id=1, source_target_pairs={{0,13},{1,12},{2,15},{3,14},{4,9},{5,8},{6,11},{7,10},{8,5},{9,4},... | collective-permute-start | bytes 30728 | tf_op jit(solution)/shard_map/ppermute | solution.py:583
  23.3 4.2 %collective-permute-start.11 = (bf16[8,640]{1,0:T(8,128)(2,1)S(1)}, bf16[8,640]{1,0:T(8,128)(2,1)S(1)}, u32[]{:S(2)}, u32[]{:S(2)}) collective-permute-start(bf16[8,640]{1,0:T(8,128)(2,1)S(1)} %get-tuple-element.64), channel_id=1, source_target_pairs={{0,9},{1,8},{2,11},{3,10},{4,13},{5,12},{6,15},{7,14},{8,1},{9,0},... | collective-permute-start | bytes 30728 | tf_op jit(solution)/shard_map/ppermute | solution.py:583
  24.1 3.4 %collective-permute-start.12 = (bf16[8,640]{1,0:T(8,128)(2,1)S(1)}, bf16[8,640]{1,0:T(8,128)(2,1)S(1)}, u32[]{:S(2)}, u32[]{:S(2)}) collective-permute-start(bf16[8,640]{1,0:T(8,128)(2,1)S(1)} %get-tuple-element.65), channel_id=1, source_target_pairs={{0,5},{1,4},{2,7},{3,6},{4,1},{5,0},{6,3},{7,2},{8,13},{9,12},{10,... | collective-permute-start | bytes 30728 | tf_op jit(solution)/shard_map/ppermute | solution.py:583
  25.6 1.9 %collective-permute-start.9 = (bf16[8,640]{1,0:T(8,128)(2,1)S(1)}, bf16[8,640]{1,0:T(8,128)(2,1)S(1)}, u32[]{:S(2)}, u32[]{:S(2)}) collective-permute-start(bf16[8,640]{1,0:T(8,128)(2,1)S(1)} %get-tuple-element.55.fresh_ref), channel_id=1, source_target_pairs={{0,1},{1,0},{2,3},{3,2},{4,5},{5,4},{6,7},{7,6},{8,9},{9,8},{10,11... | collective-permute-start | bytes 30728 | tf_op jit(solution)/shard_map/ppermute | solution.py:587
  28.0 3.4 %copy-start = (bf16[1024,2048]{1,0:T(8,128)(2,1)S(1)}, bf16[1024,2048]{1,0:T(8,128)(2,1)}, u32[]{:S(2)}) copy-start(bf16[1024,2048]{1,0:T(8,128)(2,1)} %up_ref.1) | copy-start | bytes 12582916
  28.0 3.4 %copy-start.5 = (f32[1024]{0:T(1024)S(1)}, f32[1024]{0:T(1024)}, u32[]{:S(2)}) copy-start(f32[1024]{0:T(1024)} %param.16) | copy-start | bytes 12292
  28.0 3.4 %collective-permute-start.13 = (bf16[16,1024]{1,0:T(8,128)(2,1)S(1)}, bf16[16,1024]{1,0:T(8,128)(2,1)S(1)}, u32[]{:S(2)}, u32[]{:S(2)}) collective-permute-start(bf16[16,1024]{1,0:T(8,128)(2,1)S(1)} %get-tuple-element.71.after_ref), channel_id=1, source_target_pairs={{0,17},{1,16},{2,19},{3,18},{4,21},{5,20},{6,23},{7,22},{8,25},{9,... | collective-permute-start | bytes 98312 | tf_op jit(solution)/shard_map/ppermute | solution.py:606
  32.7 3.2 %collective-permute-start.15 = (f32[8,512]{1,0:T(8,128)S(1)}, f32[8,512]{1,0:T(8,128)S(1)}, u32[]{:S(2)}, u32[]{:S(2)}) collective-permute-start(f32[8,512]{1,0:T(8,128)S(1)} %get-tuple-element.74), channel_id=1, source_target_pairs={{0,16},{1,17},{2,18},{3,19},{4,20},{5,21},{6,22},{7,23},{8,24},{9,... | collective-permute-start | bytes 49160 | tf_op jit(solution)/shard_map/ppermute | solution.py:623
  34.3 1.6 %collective-permute-start.14 = (f32[8,512]{1,0:T(8,128)S(1)}, f32[8,512]{1,0:T(8,128)S(1)}, u32[]{:S(2)}, u32[]{:S(2)}) collective-permute-start(f32[8,512]{1,0:T(8,128)S(1)} %get-tuple-element.73), channel_id=1, source_target_pairs={{0,1},{1,0},{2,3},{3,2},{4,5},{5,4},{6,7},{7,6},{8,9},{9,8},{10,11... | collective-permute-start | bytes 49160 | tf_op jit(solution)/shard_map/ppermute | solution.py:624

commit v2 on v0

--- a/solution.py
+++ b/solution.py
@@ -466,7 +466,7 @@
         for step in range(1, blocks // inner)
     ]
     depth = page_count * PIECE
-    early = page_count // 6 * 2
+    early = page_count // 12 * 2
     keys, picks, place, leads, apart, owners = pl.pallas_call(
         functools.partial(page_kernel, own_rows, inner, blocks // inner, exchanged),
         out_shape=(

time: 36.7 us -> 36.7 us (level)
  transfers between devices with their start and end apart: 16 -> 16, of which waited for: 6 -> 5; matrix products, arithmetic and copies ran while one was open for 0% -> 0% of each run, Pallas kernels for 23% -> 23%
where the time goes in v2:
time: 36.7 us; the launch traced here: 36.5 us
  starting transfers between devices  17 us (46%)
  Pallas kernels  13.7 us (37%)
  waiting for transfers between devices  5.02 us (14%)
  other arithmetic  0.61 us (2%)
    ppermute x3, starting transfers between devices, per_device(): lax.ppermute(query, 'blk', xor_pairs(blocks, step * inner ^ 1))  5.48 us
    ppermute x3, starting transfers between devices, per_device(): lax.ppermute(sums[step], 'blk', xor_pairs(blocks, step * inner ^ 1))  3.89 us
    pallas_call x2, Pallas kernels, load_down(): pl.pallas_call(functools.partial(load_kernel, start), out_shape=pltpu.VME...  3.1 us
    pallas_call x1, Pallas kernels, per_device(): pl.pallas_call(side_kernel, out_shape=(shape((own_rows, width + LANES), b...  2.17 us
    ppermute x3, starting transfers between devices, per_device(): lax.ppermute(sums[i], 'blk', xor_pairs(blocks, steps[i]))  2.17 us
    ppermute x3, starting transfers between devices, per_device(): lax.ppermute(near, 'blk', xor_pairs(blocks, step))  2.14 us
    ppermute x3, waiting for transfers between devices, per_device(): lax.ppermute(query, 'blk', xor_pairs(blocks, step * inner ^ 1))  1.8 us
    pallas_call x1, Pallas kernels, per_device(): pl.pallas_call(functools.partial(attend_kernel, groups), out_shape=(shape...  1.78 us
  transfers between devices with their start and end apart: 16, of which 5 were waited for; matrix products, arithmetic and copies ran while one was open for 0% of the time, Pallas kernels for 23%

profile of v2, /device:TPU:0, one launch (start us, length us, event | category | flops | bytes accessed | tf_op | source)
XLA Modules:
  0.0 36.5 jit_solution(17371216885261695016)
XLA Ops:
  0.0 0.0 copy-start.6
  0.0 1.4 %query.1.query_ref = bf16[8,512]{1,0:T(8,128)(2,1)S(1)} custom-call(f32[8,1024]{1,0:T(8,128)} %hidden_ref.3, f32[1,1024]{1,0:T(1,128)} %bitcast.6, bf16[3,1024,512]{2,1,0:T(8,128)(2,1)} %weight_hbm.3), custom_call_target="tpu_custom_call" | custom-call | tf_op jit(solution)/shard_map/query/pallas_call | solution.py:446
  1.4 4.6 %collective-permute-start.2 = (bf16[8,512]{1,0:T(8,128)(2,1)S(1)}, bf16[8,512]{1,0:T(8,128)(2,1)S(1)}, u32[]{:S(2)}, u32[]{:S(2)}) collective-permute-start(bf16[8,512]{1,0:T(8,128)(2,1)S(1)} %query.1.query_ref), channel_id=1, source_target_pairs={{0,13},{1,12},{2,15},{3,14},{4,9},{5,8},{6,11},{7,10},{8,5},{9,4},... | collective-permute-start | bytes 24584 | tf_op jit(solution)/shard_map/ppermute | solution.py:465
  6.0 0.0 collective-permute-start.1
  6.0 0.9 %collective-permute-start = (bf16[8,512]{1,0:T(8,128)(2,1)S(1)}, bf16[8,512]{1,0:T(8,128)(2,1)S(1)}, u32[]{:S(2)}, u32[]{:S(2)}) collective-permute-start(bf16[8,512]{1,0:T(8,128)(2,1)S(1)} %query.1.query_ref), channel_id=1, source_target_pairs={{0,5},{1,4},{2,7},{3,6},{4,1},{5,0},{6,3},{7,2},{8,13},{9,12},{10,... | collective-permute-start | bytes 24584 | tf_op jit(solution)/shard_map/ppermute | solution.py:465
  6.9 0.0 copy-done.6
  6.9 0.0 copy-start.1
  6.9 1.3 %pages.1 = (bf16[4,128,512]{2,1,0:T(8,128)(2,1)S(1)}, bf16[192,128]{1,0:T(8,128)(2,1)S(1)}, bf16[128,192]{1,0:T(8,128)(2,1)S(1)}, f32[24,128]{1,0:T(8,128)S(1)},...) custom-call(bf16[8,512]{1,0:T(8,128)(2,1)S(1)} %query.1.query_ref, s32[1,24]{1,0:T(1,128)S(1)} %bitcast.11, ...), custom_call_target="tpu_custom_call" | custom-call | bytes 3145728 | tf_op jit(solution)/shard_map/pages/pallas_call | solution.py:470
  8.2 0.0 collective-permute-done.2
  8.2 1.8 %collective-permute-done.1 = bf16[8,512]{1,0:T(8,128)(2,1)S(1)} collective-permute-done((bf16[8,512]{1,0:T(8,128)(2,1)S(1)}, bf16[8,512]{1,0:T(8,128)(2,1)S(1)}, u32[]{:S(2)}, u32[]{:S(2)}) %collective-permute-start.1) | collective-permute-done | bytes 8224 | tf_op jit(solution)/shard_map/ppermute | solution.py:465
  10.0 0.0 collective-permute-done
  10.0 1.5 %collective-permute-start.3 = (bf16[32,512]{1,0:T(8,128)(2,1)S(1)}, bf16[32,512]{1,0:T(8,128)(2,1)S(1)}, u32[]{:S(2)}, u32[]{:S(2)}) collective-permute-start(bf16[32,512]{1,0:T(8,128)(2,1)S(1)} %pad_maximum_fusion.after_ref.refs_0_), channel_id=1, source_target_pairs={{0,2},{1,3},{2,0},{3,1},{4,6},{5,7},{6,4},{7,5},{8,10},{9,11},{10,... | collective-permute-start | bytes 98312 | tf_op jit(solution)/shard_map/ppermute | solution.py:489
  11.5 0.5 %collective-permute-start.4 = (bf16[32,512]{1,0:T(8,128)(2,1)S(1)}, bf16[32,512]{1,0:T(8,128)(2,1)S(1)}, u32[]{:S(2)}, u32[]{:S(2)}) collective-permute-start(bf16[32,512]{1,0:T(8,128)(2,1)S(1)} %pad_maximum_fusion.after_ref.refs_0_), channel_id=1, source_target_pairs={{0,3},{1,2},{2,1},{3,0},{4,7},{5,6},{6,5},{7,4},{8,11},{9,10},{10,... | collective-permute-start | bytes 98312 | tf_op jit(solution)/shard_map/ppermute | solution.py:489
  12.0 0.2 collective-permute-start.5
  12.2 1.8 %bias.1 = (bf16[20,128,512]{2,1,0:T(8,128)(2,1)S(1)}, f32[192,128]{1,0:T(8,128)S(1)}) custom-call(f32[8,32]{1,0:T(8,128)} %bitcast.8, s32[31]{0:T(128)} %edges_hbm.1, s32[1,128]{1,0:T(1,128)} %bitcast.12, s32[1,24]{1,0:T(1,128)} %bitcast.13, s32[24,128]{1,0:T(8,128)S(1)} %get-tuple-element.42.owners_ref, bf16[24,128,512]{2,1,0:T(8,128)(2,1)} %keys_hbm.3, ...), custom_call_target="tpu_custom_call" | custom-call | bytes 3145728 | tf_op jit(solution)/shard_map/bias/pallas_call | solution.py:491
  14.0 0.0 collective-permute-done.3.refs_1_
  14.0 0.9 %collective-permute-done.4.refs_2_ = bf16[32,512]{1,0:T(8,128)(2,1)S(1)} collective-permute-done((bf16[32,512]{1,0:T(8,128)(2,1)S(1)}, bf16[32,512]{1,0:T(8,128)(2,1)S(1)}, u32[]{:S(2)}, u32[]{:S(2)}) %collective-permute-start.4) | collective-permute-done | bytes 32800 | tf_op jit(solution)/shard_map/ppermute | solution.py:489
  14.9 0.0 collective-permute-done.5.refs_3_
  14.9 0.0 copy-done.1
  14.9 0.0 copy-start.2
  14.9 0.0 copy-start.3
  14.9 0.0 copy-start.4
  14.9 1.8 %attend.1 = (bf16[144,128]{1,0:T(8,128)(2,1)S(1)}, bf16[144,128]{1,0:T(8,128)(2,1)S(1)}, bf16[144,128]{1,0:T(8,128)(2,1)S(1)}, bf16[144,128]{1,0:T(8,128)(2,1)S(1)}) custom-call(bf16[32,512]{1,0:T(8,128)(2,1)S(1)} %pad_maximum_fusion.after_ref.refs_0_, bf16[32,512]{1,0:T(8,128)(2,1)S(1)} %collective-permute-done.3.refs_1_, ...), custom_call_target="tpu_custom_call" | custom-call | tf_op jit(solution)/shard_map/attend/pallas_call | solution.py:518
  16.7 1.0 %collective-permute-start.6 = (bf16[144,128]{1,0:T(8,128)(2,1)S(1)}, bf16[144,128]{1,0:T(8,128)(2,1)S(1)}, u32[]{:S(2)}, u32[]{:S(2)}) collective-permute-start(bf16[144,128]{1,0:T(8,128)(2,1)S(1)} %get-tuple-element.51), channel_id=1, source_target_pairs={{0,2},{1,3},{2,0},{3,1},{4,6},{5,7},{6,4},{7,5},{8,10},{9,11},{10,... | collective-permute-start | bytes 110600 | tf_op jit(solution)/shard_map/ppermute | solution.py:527
  17.7 0.8 %collective-permute-start.7 = (bf16[144,128]{1,0:T(8,128)(2,1)S(1)}, bf16[144,128]{1,0:T(8,128)(2,1)S(1)}, u32[]{:S(2)}, u32[]{:S(2)}) collective-permute-start(bf16[144,128]{1,0:T(8,128)(2,1)S(1)} %get-tuple-element.52), channel_id=1, source_target_pairs={{0,3},{1,2},{2,1},{3,0},{4,7},{5,6},{6,5},{7,4},{8,11},{9,10},{10,... | collective-permute-start | bytes 110600 | tf_op jit(solution)/shard_map/ppermute | solution.py:527
  18.4 0.4 %collective-permute-start.8 = (bf16[144,128]{1,0:T(8,128)(2,1)S(1)}, bf16[144,128]{1,0:T(8,128)(2,1)S(1)}, u32[]{:S(2)}, u32[]{:S(2)}) collective-permute-start(bf16[144,128]{1,0:T(8,128)(2,1)S(1)} %get-tuple-element.53), channel_id=1, source_target_pairs={{0,1},{1,0},{2,3},{3,2},{4,5},{5,4},{6,7},{7,6},{8,9},{9,8},{10,11... | collective-permute-start | bytes 110600 | tf_op jit(solution)/shard_map/ppermute | solution.py:527
  18.9 0.0 copy-done.2
  18.9 0.0 copy-done.3
  18.9 0.0 copy-done.4
  18.9 2.2 %side.1 = (bf16[8,640]{1,0:T(8,128)(2,1)S(1)}, bf16[512,1024]{1,0:T(8,128)(2,1)S(1)}, bf16[256,512]{1,0:T(8,128)(2,1)S(1)}) custom-call(f32[8,1024]{1,0:T(8,128)S(1)} %copy-done.2, f32[1,1024]{1,0:T(1,128)S(1)} %bitcast.7, bf16[8,512]{1,0:T(8,128)(2,1)S(1)} %query.1.query_ref, f32[8,32]{1,0:T(8,128)S(1)} %bitcast.9, bf16[3,1024,512]{2,1,0:T(8,128)(2,1)} %weight_hbm.3, ...), custom_call_target="tpu_custom_call" | custom-call | bytes 3145728 | tf_op jit(solution)/shard_map/side/pallas_call | solution.py:531
  21.0 0.0 collective-permute-done.6.refs_1_
  21.1 0.3 collective-permute-done.7.refs_2_
  21.3 0.0 collective-permute-done.8.refs_3_
  21.3 0.4 %combine.1 = (bf16[8,640]{1,0:T(8,128)(2,1)S(1)}, bf16[8,640]{1,0:T(8,128)(2,1)S(1)}, bf16[8,640]{1,0:T(8,128)(2,1)S(1)}, bf16[8,640]{1,0:T(8,128)(2,1)S(1)}) custom-call(bf16[144,128]{1,0:T(8,128)(2,1)S(1)} %get-tuple-element.58.after_ref.refs_0_, bf16[144,128]{1,0:T(8,128)(2,1)S(1)} %collective-permute-done.6.refs_1_, ...), custom_call_target="tpu_custom_call" | custom-call | tf_op jit(solution)/shard_map/combine/pallas_call | solution.py:555
  21.7 1.4 %collective-permute-start.10 = (bf16[8,640]{1,0:T(8,128)(2,1)S(1)}, bf16[8,640]{1,0:T(8,128)(2,1)S(1)}, u32[]{:S(2)}, u32[]{:S(2)}) collective-permute-start(bf16[8,640]{1,0:T(8,128)(2,1)S(1)} %get-tuple-element.63), channel_id=1, source_target_pairs={{0,13},{1,12},{2,15},{3,14},{4,9},{5,8},{6,11},{7,10},{8,5},{9,4},... | collective-permute-start | bytes 30728 | tf_op jit(solution)/shard_map/ppermute | solution.py:580
  23.2 0.9 %collective-permute-start.11 = (bf16[8,640]{1,0:T(8,128)(2,1)S(1)}, bf16[8,640]{1,0:T(8,128)(2,1)S(1)}, u32[]{:S(2)}, u32[]{:S(2)}) collective-permute-start(bf16[8,640]{1,0:T(8,128)(2,1)S(1)} %get-tuple-element.64), channel_id=1, source_target_pairs={{0,9},{1,8},{2,11},{3,10},{4,13},{5,12},{6,15},{7,14},{8,1},{9,0},... | collective-permute-start | bytes 30728 | tf_op jit(solution)/shard_map/ppermute | solution.py:580
  24.1 1.5 %collective-permute-start.12 = (bf16[8,640]{1,0:T(8,128)(2,1)S(1)}, bf16[8,640]{1,0:T(8,128)(2,1)S(1)}, u32[]{:S(2)}, u32[]{:S(2)}) collective-permute-start(bf16[8,640]{1,0:T(8,128)(2,1)S(1)} %get-tuple-element.65), channel_id=1, source_target_pairs={{0,5},{1,4},{2,7},{3,6},{4,1},{5,0},{6,3},{7,2},{8,13},{9,12},{10,... | collective-permute-start | bytes 30728 | tf_op jit(solution)/shard_map/ppermute | solution.py:580
  25.6 0.4 %collective-permute-start.9 = (bf16[8,640]{1,0:T(8,128)(2,1)S(1)}, bf16[8,640]{1,0:T(8,128)(2,1)S(1)}, u32[]{:S(2)}, u32[]{:S(2)}) collective-permute-start(bf16[8,640]{1,0:T(8,128)(2,1)S(1)} %get-tuple-element.55.fresh_ref), channel_id=1, source_target_pairs={{0,1},{1,0},{2,3},{3,2},{4,5},{5,4},{6,7},{7,6},{8,9},{9,8},{10,11... | collective-permute-start | bytes 30728 | tf_op jit(solution)/shard_map/ppermute | solution.py:584
  26.1 1.4 %load.2.down_ref = bf16[768,1024]{1,0:T(8,128)(2,1)S(1)} custom-call(bf16[2048,1024]{1,0:T(8,128)(2,1)} %source.3, bf16[8,640]{1,0:T(8,128)(2,1)S(1)} %get-tuple-element.66.after_ref.refs_0_), custom_call_target="tpu_custom_call" | custom-call | bytes 4194304 | tf_op jit(solution)/shard_map/load/pallas_call | solution.py:567
  27.4 0.0 collective-permute-done.10.refs_1_
  27.5 0.0 collective-permute-done.11.refs_2_
  27.5 0.0 collective-permute-done.12.refs_3_
  27.5 0.0 collective-permute-done.9.moved_ref
  27.5 0.5 %merge.1 = (f32[8,1024]{1,0:T(8,128)S(1)}, bf16[16,1024]{1,0:T(8,128)(2,1)S(1)}) custom-call(f32[8,1024]{1,0:T(8,128)S(1)} %copy-done.2, bf16[8,640]{1,0:T(8,128)(2,1)S(1)} %get-tuple-element.55.fresh_ref, bf16[8,640]{1,0:T(8,128)(2,1)S(1)} %collective-permute-done.9.moved_ref, bf16[512,1024]{1,0:T(8,128)(2,1)S(1)} %get-tuple-element.56.weight_ref, ...), custom_call_target="tpu_custom_call" | custom-call | tf_op jit(solution)/shard_map/merge/pallas_call | solution.py:586
  28.0 0.0 copy-start
  28.0 0.0 copy-start.5
  28.0 1.3 %collective-permute-start.13 = (bf16[16,1024]{1,0:T(8,128)(2,1)S(1)}, bf16[16,1024]{1,0:T(8,128)(2,1)S(1)}, u32[]{:S(2)}, u32[]{:S(2)}) collective-permute-start(bf16[16,1024]{1,0:T(8,128)(2,1)S(1)} %get-tuple-element.71.after_ref), channel_id=1, source_target_pairs={{0,17},{1,16},{2,19},{3,18},{4,21},{5,20},{6,23},{7,22},{8,25},{9,... | collective-permute-start | bytes 98312 | tf_op jit(solution)/shard_map/ppermute | solution.py:603
  29.4 1.7 %load.3.late_ref = bf16[1280,1024]{1,0:T(8,128)(2,1)S(1)} custom-call(bf16[2048,1024]{1,0:T(8,128)(2,1)} %source.3, bf16[16,1024]{1,0:T(8,128)(2,1)S(1)} %get-tuple-element.71.after_ref), custom_call_target="tpu_custom_call" | custom-call | bytes 4194304 | tf_op jit(solution)/shard_map/load/pallas_call | solution.py:567
  31.1 0.4 %collective-permute-done.13.other_ref = bf16[16,1024]{1,0:T(8,128)(2,1)S(1)} collective-permute-done((bf16[16,1024]{1,0:T(8,128)(2,1)S(1)}, bf16[16,1024]{1,0:T(8,128)(2,1)S(1)}, u32[]{:S(2)}, u32[]{:S(2)}) %collective-permute-start.13) | collective-permute-done | bytes 32800 | tf_op jit(solution)/shard_map/ppermute | solution.py:603
  31.5 0.0 copy-done
  31.5 0.0 copy-done.5
  31.5 1.3 %mlp.1 = (f32[8,512]{1,0:T(8,128)S(1)}, f32[8,512]{1,0:T(8,128)S(1)}) custom-call(f32[8,1024]{1,0:T(8,128)S(1)} %get-tuple-element.70.own_ref, bf16[16,1024]{1,0:T(8,128)(2,1)S(1)} %collective-permute-done.13.other_ref, f32[1,1024]{1,0:T(1,128)S(1)} %bitcast.10, bf16[1024,2048]{1,0:T(8,128)(2,1)S(1)} %copy-done, bf16[768,1024]{1,0:T(8,128)(2,1)S(1)} %load.2.down_ref, ...), custom_call_target="tpu_custom_call" | custom-call | tf_op jit(solution)/shard_map/mlp/pallas_call | solution.py:609
  32.7 1.5 %collective-permute-start.15 = (f32[8,512]{1,0:T(8,128)S(1)}, f32[8,512]{1,0:T(8,128)S(1)}, u32[]{:S(2)}, u32[]{:S(2)}) collective-permute-start(f32[8,512]{1,0:T(8,128)S(1)} %get-tuple-element.74), channel_id=1, source_target_pairs={{0,16},{1,17},{2,18},{3,19},{4,20},{5,21},{6,22},{7,23},{8,24},{9,... | collective-permute-start | bytes 49160 | tf_op jit(solution)/shard_map/ppermute | solution.py:620
  34.3 0.0 collective-permute-start.14
  34.3 1.6 %collective-permute-done.15 = f32[8,512]{1,0:T(8,128)S(1)} collective-permute-done((f32[8,512]{1,0:T(8,128)S(1)}, f32[8,512]{1,0:T(8,128)S(1)}, u32[]{:S(2)}, u32[]{:S(2)}) %collective-permute-start.15) | collective-permute-done | bytes 16416 | tf_op jit(solution)/shard_map/ppermute | solution.py:620
  35.9 0.0 collective-permute-done.14
  35.9 0.6 %select_add_fusion = f32[8,512]{1,0:T(8,128)} fusion(f32[8,512]{1,0:T(8,128)S(1)} %collective-permute-done.15, f32[8,512]{1,0:T(8,128)S(1)} %get-tuple-element.73, f32[8,512]{1,0:T(8,128)S(1)} %collective-permute-done.14, pred[]{:T(512)S(6)} %eq.3), kind=kLoop, calls=%fused_computation.1 | loop fusion | flops 8192 | bytes 65537 | tf_op jit(solution)/shard_map/add | solution.py:626
  (1 shorter events, 0.0 us)
Async XLA Ops:
  0.0 6.9 %copy-start.6 = (s32[24]{0:T(128)S(1)}, s32[24]{0:T(128)}, u32[]{:S(2)}) copy-start(s32[24]{0:T(128)} %param.26) | copy-start | bytes 292
  1.4 6.8 %collective-permute-start.2 = (bf16[8,512]{1,0:T(8,128)(2,1)S(1)}, bf16[8,512]{1,0:T(8,128)(2,1)S(1)}, u32[]{:S(2)}, u32[]{:S(2)}) collective-permute-start(bf16[8,512]{1,0:T(8,128)(2,1)S(1)} %query.1.query_ref), channel_id=1, source_target_pairs={{0,13},{1,12},{2,15},{3,14},{4,9},{5,8},{6,11},{7,10},{8,5},{9,4},... | collective-permute-start | bytes 24584 | tf_op jit(solution)/shard_map/ppermute | solution.py:465
  6.0 4.0 %collective-permute-start.1 = (bf16[8,512]{1,0:T(8,128)(2,1)S(1)}, bf16[8,512]{1,0:T(8,128)(2,1)S(1)}, u32[]{:S(2)}, u32[]{:S(2)}) collective-permute-start(bf16[8,512]{1,0:T(8,128)(2,1)S(1)} %query.1.query_ref), channel_id=1, source_target_pairs={{0,9},{1,8},{2,11},{3,10},{4,13},{5,12},{6,15},{7,14},{8,1},{9,0},... | collective-permute-start | bytes 24584 | tf_op jit(solution)/shard_map/ppermute | solution.py:465
  6.0 4.0 %collective-permute-start = (bf16[8,512]{1,0:T(8,128)(2,1)S(1)}, bf16[8,512]{1,0:T(8,128)(2,1)S(1)}, u32[]{:S(2)}, u32[]{:S(2)}) collective-permute-start(bf16[8,512]{1,0:T(8,128)(2,1)S(1)} %query.1.query_ref), channel_id=1, source_target_pairs={{0,5},{1,4},{2,7},{3,6},{4,1},{5,0},{6,3},{7,2},{8,13},{9,12},{10,... | collective-permute-start | bytes 24584 | tf_op jit(solution)/shard_map/ppermute | solution.py:465
  6.9 7.9 %copy-start.1 = (bf16[24,128,512]{2,1,0:T(8,128)(2,1)S(1)}, bf16[24,128,512]{2,1,0:T(8,128)(2,1)}, u32[]{:S(2)}) copy-start(bf16[24,128,512]{2,1,0:T(8,128)(2,1)} %refs_11_.1) | copy-start | bytes 9437188
  10.0 3.9 %collective-permute-start.3 = (bf16[32,512]{1,0:T(8,128)(2,1)S(1)}, bf16[32,512]{1,0:T(8,128)(2,1)S(1)}, u32[]{:S(2)}, u32[]{:S(2)}) collective-permute-start(bf16[32,512]{1,0:T(8,128)(2,1)S(1)} %pad_maximum_fusion.after_ref.refs_0_), channel_id=1, source_target_pairs={{0,2},{1,3},{2,0},{3,1},{4,6},{5,7},{6,4},{7,5},{8,10},{9,11},{10,... | collective-permute-start | bytes 98312 | tf_op jit(solution)/shard_map/ppermute | solution.py:489
  11.5 3.3 %collective-permute-start.4 = (bf16[32,512]{1,0:T(8,128)(2,1)S(1)}, bf16[32,512]{1,0:T(8,128)(2,1)S(1)}, u32[]{:S(2)}, u32[]{:S(2)}) collective-permute-start(bf16[32,512]{1,0:T(8,128)(2,1)S(1)} %pad_maximum_fusion.after_ref.refs_0_), channel_id=1, source_target_pairs={{0,3},{1,2},{2,1},{3,0},{4,7},{5,6},{6,5},{7,4},{8,11},{9,10},{10,... | collective-permute-start | bytes 98312 | tf_op jit(solution)/shard_map/ppermute | solution.py:489
  12.0 2.9 %collective-permute-start.5 = (bf16[32,512]{1,0:T(8,128)(2,1)S(1)}, bf16[32,512]{1,0:T(8,128)(2,1)S(1)}, u32[]{:S(2)}, u32[]{:S(2)}) collective-permute-start(bf16[32,512]{1,0:T(8,128)(2,1)S(1)} %pad_maximum_fusion.after_ref.refs_0_), channel_id=1, source_target_pairs={{0,1},{1,0},{2,3},{3,2},{4,5},{5,4},{6,7},{7,6},{8,9},{9,8},{10,11... | collective-permute-start | bytes 98312 | tf_op jit(solution)/shard_map/ppermute | solution.py:489
  14.9 4.0 %copy-start.2 = (f32[8,1024]{1,0:T(8,128)S(1)}, f32[8,1024]{1,0:T(8,128)}, u32[]{:S(2)}) copy-start(f32[8,1024]{1,0:T(8,128)} %hidden_ref.3) | copy-start | bytes 98308
  14.9 4.0 %copy-start.3 = (f32[1024]{0:T(1024)S(1)}, f32[1024]{0:T(1024)}, u32[]{:S(2)}) copy-start(f32[1024]{0:T(1024)} %param.15) | copy-start | bytes 12292
  14.9 4.0 %copy-start.4 = (f32[32,8]{0,1:T(8,128)S(1)}, f32[32,8]{0,1:T(8,128)}, u32[]{:S(2)}) copy-start(f32[32,8]{0,1:T(8,128)} %param.21) | copy-start | bytes 3076
  16.7 4.4 %collective-permute-start.6 = (bf16[144,128]{1,0:T(8,128)(2,1)S(1)}, bf16[144,128]{1,0:T(8,128)(2,1)S(1)}, u32[]{:S(2)}, u32[]{:S(2)}) collective-permute-start(bf16[144,128]{1,0:T(8,128)(2,1)S(1)} %get-tuple-element.51), channel_id=1, source_target_pairs={{0,2},{1,3},{2,0},{3,1},{4,6},{5,7},{6,4},{7,5},{8,10},{9,11},{10,... | collective-permute-start | bytes 110600 | tf_op jit(solution)/shard_map/ppermute | solution.py:527
  17.7 3.7 %collective-permute-start.7 = (bf16[144,128]{1,0:T(8,128)(2,1)S(1)}, bf16[144,128]{1,0:T(8,128)(2,1)S(1)}, u32[]{:S(2)}, u32[]{:S(2)}) collective-permute-start(bf16[144,128]{1,0:T(8,128)(2,1)S(1)} %get-tuple-element.52), channel_id=1, source_target_pairs={{0,3},{1,2},{2,1},{3,0},{4,7},{5,6},{6,5},{7,4},{8,11},{9,10},{10,... | collective-permute-start | bytes 110600 | tf_op jit(solution)/shard_map/ppermute | solution.py:527
  18.4 2.9 %collective-permute-start.8 = (bf16[144,128]{1,0:T(8,128)(2,1)S(1)}, bf16[144,128]{1,0:T(8,128)(2,1)S(1)}, u32[]{:S(2)}, u32[]{:S(2)}) collective-permute-start(bf16[144,128]{1,0:T(8,128)(2,1)S(1)} %get-tuple-element.53), channel_id=1, source_target_pairs={{0,1},{1,0},{2,3},{3,2},{4,5},{5,4},{6,7},{7,6},{8,9},{9,8},{10,11... | collective-permute-start | bytes 110600 | tf_op jit(solution)/shard_map/ppermute | solution.py:527
  21.7 5.7 %collective-permute-start.10 = (bf16[8,640]{1,0:T(8,128)(2,1)S(1)}, bf16[8,640]{1,0:T(8,128)(2,1)S(1)}, u32[]{:S(2)}, u32[]{:S(2)}) collective-permute-start(bf16[8,640]{1,0:T(8,128)(2,1)S(1)} %get-tuple-element.63), channel_id=1, source_target_pairs={{0,13},{1,12},{2,15},{3,14},{4,9},{5,8},{6,11},{7,10},{8,5},{9,4},... | collective-permute-start | bytes 30728 | tf_op jit(solution)/shard_map/ppermute | solution.py:580
  23.2 4.3 %collective-permute-start.11 = (bf16[8,640]{1,0:T(8,128)(2,1)S(1)}, bf16[8,640]{1,0:T(8,128)(2,1)S(1)}, u32[]{:S(2)}, u32[]{:S(2)}) collective-permute-start(bf16[8,640]{1,0:T(8,128)(2,1)S(1)} %get-tuple-element.64), channel_id=1, source_target_pairs={{0,9},{1,8},{2,11},{3,10},{4,13},{5,12},{6,15},{7,14},{8,1},{9,0},... | collective-permute-start | bytes 30728 | tf_op jit(solution)/shard_map/ppermute | solution.py:580
  24.1 3.4 %collective-permute-start.12 = (bf16[8,640]{1,0:T(8,128)(2,1)S(1)}, bf16[8,640]{1,0:T(8,128)(2,1)S(1)}, u32[]{:S(2)}, u32[]{:S(2)}) collective-permute-start(bf16[8,640]{1,0:T(8,128)(2,1)S(1)} %get-tuple-element.65), channel_id=1, source_target_pairs={{0,5},{1,4},{2,7},{3,6},{4,1},{5,0},{6,3},{7,2},{8,13},{9,12},{10,... | collective-permute-start | bytes 30728 | tf_op jit(solution)/shard_map/ppermute | solution.py:580
  25.6 1.9 %collective-permute-start.9 = (bf16[8,640]{1,0:T(8,128)(2,1)S(1)}, bf16[8,640]{1,0:T(8,128)(2,1)S(1)}, u32[]{:S(2)}, u32[]{:S(2)}) collective-permute-start(bf16[8,640]{1,0:T(8,128)(2,1)S(1)} %get-tuple-element.55.fresh_ref), channel_id=1, source_target_pairs={{0,1},{1,0},{2,3},{3,2},{4,5},{5,4},{6,7},{7,6},{8,9},{9,8},{10,11... | collective-permute-start | bytes 30728 | tf_op jit(solution)/shard_map/ppermute | solution.py:584
  28.0 3.5 %copy-start = (bf16[1024,2048]{1,0:T(8,128)(2,1)S(1)}, bf16[1024,2048]{1,0:T(8,128)(2,1)}, u32[]{:S(2)}) copy-start(bf16[1024,2048]{1,0:T(8,128)(2,1)} %up_ref.1) | copy-start | bytes 12582916
  28.0 3.5 %copy-start.5 = (f32[1024]{0:T(1024)S(1)}, f32[1024]{0:T(1024)}, u32[]{:S(2)}) copy-start(f32[1024]{0:T(1024)} %param.16) | copy-start | bytes 12292
  28.0 3.4 %collective-permute-start.13 = (bf16[16,1024]{1,0:T(8,128)(2,1)S(1)}, bf16[16,1024]{1,0:T(8,128)(2,1)S(1)}, u32[]{:S(2)}, u32[]{:S(2)}) collective-permute-start(bf16[16,1024]{1,0:T(8,128)(2,1)S(1)} %get-tuple-element.71.after_ref), channel_id=1, source_target_pairs={{0,17},{1,16},{2,19},{3,18},{4,21},{5,20},{6,23},{7,22},{8,25},{9,... | collective-permute-start | bytes 98312 | tf_op jit(solution)/shard_map/ppermute | solution.py:603
  32.7 3.2 %collective-permute-start.15 = (f32[8,512]{1,0:T(8,128)S(1)}, f32[8,512]{1,0:T(8,128)S(1)}, u32[]{:S(2)}, u32[]{:S(2)}) collective-permute-start(f32[8,512]{1,0:T(8,128)S(1)} %get-tuple-element.74), channel_id=1, source_target_pairs={{0,16},{1,17},{2,18},{3,19},{4,20},{5,21},{6,22},{7,23},{8,24},{9,... | collective-permute-start | bytes 49160 | tf_op jit(solution)/shard_map/ppermute | solution.py:620
  34.3 1.7 %collective-permute-start.14 = (f32[8,512]{1,0:T(8,128)S(1)}, f32[8,512]{1,0:T(8,128)S(1)}, u32[]{:S(2)}, u32[]{:S(2)}) collective-permute-start(f32[8,512]{1,0:T(8,128)S(1)} %get-tuple-element.73), channel_id=1, source_target_pairs={{0,1},{1,0},{2,3},{3,2},{4,5},{5,4},{6,7},{7,6},{8,9},{9,8},{10,11... | collective-permute-start | bytes 49160 | tf_op jit(solution)/shard_map/ppermute | solution.py:621
